TPU v7x, 256 devices: a whole 4x4x8 slice. The times are simulated.
256 devices in a mesh: dp: 64 (over x, z, core), mp: 4 (over y).
Axes of the slice: x: 4, y: 4, z: 8, core: 2. Of those that a mesh axis runs over, the one named last changes fastest.
Arguments:
- grad_in: bfloat16 [64, 192, 12288], P('dp', None, 'mp'), may hold values from -400000 to 400000
- grad_out: bfloat16 [64, 192, 12288], P('dp', None, 'mp'), may hold values from -400000 to 400000
- error_in: float32 [64, 192, 12288], P('dp', None, 'mp'), may hold values from -6 to 6
- error_out: float32 [64, 192, 12288], P('dp', None, 'mp'), may hold values from -6 to 6
- warm_in: float32 [192, 64], replicated, may hold values from -6 to 6
- warm_out: float32 [192, 64], replicated, may hold values from -6 to 6
- loss_scale: float32 [], replicated, may hold values from 1024 to 4096
Outputs:
- new_error_in: float32 [64, 192, 12288], P('dp', None, 'mp')
- new_error_out: float32 [64, 192, 12288], P('dp', None, 'mp')
- new_warm_in: float32 [192, 64], replicated
- new_warm_out: float32 [192, 64], replicated
All inputs are finite; a program needn't handle non-finite values.
Results may differ from a plain program's by a relative error of at most 0.0003.
Values sent between devices are 32-bit elements; how exact they have to be, the bound alone decides.
A program may use at most 64 MiB of HBM per device.

v0:
```python
import jax
import jax.numpy as jnp
from jax import lax
from jax.sharding import PartitionSpec as P


def contract(left_side, right_factor, dims_left, dims_right):
    return lax.dot_general(
        left_side,
        right_factor,
        (((dims_left,), (dims_right,)), ((), ())),
        precision=lax.Precision.HIGHEST,
        preferred_element_type=jnp.float32,
    )


def prepare(grad, error, warmstart_factor, loss_scale):
    gradient_plus_residual = grad[0].astype(jnp.float32) / loss_scale + error[0]
    return (gradient_plus_residual, contract(warmstart_factor, gradient_plus_residual, 0, 0))


def orthonormal(left_product):
    reduced_product = lax.psum(left_product, "dp")
    gram_matrix = lax.psum(contract(reduced_product, reduced_product, 1, 1), "mp")
    factor_low = jnp.linalg.cholesky(gram_matrix)
    return lax.linalg.triangular_solve(factor_low, reduced_product, left_side=True, lower=True)


def finish(gradient_plus_residual, orthonormal_factor, replicas):
    reduced_product = lax.psum(
        contract(gradient_plus_residual, orthonormal_factor, 1, 1), ("dp", "mp")
    )
    new_warm = reduced_product / replicas
    update = contract(new_warm, orthonormal_factor, 1, 0)
    return ((gradient_plus_residual - update)[None], new_warm)


def per_device(grad_in, grad_out, error_in, error_out, warm_in, warm_out, loss_scale):
    replicas = lax.axis_size("dp")
    field_first, left_first = prepare(grad_in, error_in, warm_in, loss_scale)
    err_first, warm_first = finish(field_first, orthonormal(left_first), replicas)
    field_second, left_second = prepare(grad_out, error_out, warm_out, loss_scale)
    err_second, warmstart_factor_second = finish(field_second, orthonormal(left_second), replicas)
    return (err_first, err_second, warm_first, warmstart_factor_second)


def solution(mesh):
    in_specs = (
        P("dp", None, "mp"),
        P("dp", None, "mp"),
        P("dp", None, "mp"),
        P("dp", None, "mp"),
        P(),
        P(),
        P(),
    )
    out_specs = (P("dp", None, "mp"), P("dp", None, "mp"), P(), P())
    return jax.shard_map(
        per_device, mesh=mesh, in_specs=in_specs, out_specs=out_specs, check_vma=False
    )
```

profile of v0, /device:TPU:1, one launch (start us, length us, event | category | flops | bytes accessed | tf_op | source)
XLA Modules:
  0.0 518.8 jit_solution(8241405067755405417)
XLA Ops:
  7.2 0.0 copy-start
  7.2 0.0 all-reduce.8.cloned.1.call-start
  7.9 0.1 copy-done
  8.0 4.9 convolution_bitcast_fusion.1
  12.9 2.8 convolution_bitcast_fusion
  15.6 0.0 all-reduce.8.cloned.1.call-update
  15.7 0.0 all-reduce.6.cloned.1.call-start
  15.7 189.8 %all-reduce.8.cloned.1.call-done = (f32[64,3072]{1,0:T(8,128)}, f32[64,3072]{1,0:T(8,128)}) async-done(((f32[64,3072]{1,0:T(8,128)}, f32[64,3072]{1,0:T(8,128)}), (f32[64,3072]{1,0:T(8,128)}, f32[64,3072]{1,0:T(8,128)})) %all-reduce.8.cloned.1.call-update) | async-done | bytes 1572880 | tf_op jit(solution)/shard_map/psum | solution.py:23
  205.5 2.3 fusion.16
  207.8 0.8 fusion.17
  208.6 14.0 %all-reduce.2 = (f32[64,64]{0,1:T(8,128)S(1)}, f32[64,64]{0,1:T(8,128)S(1)}) all-reduce(f32[64,64]{0,1:T(8,128)S(1)} %fusion.16, f32[64,64]{0,1:T(8,128)S(1)} %fusion.17), channel_id=1, replica_groups=mesh['dp'=64,'mp'=4] {'mp'}, use_global_device_ids=true, to_apply=%region_1.0 | all-reduce | flops 8192 | bytes 65536 | tf_op jit(solution)/shard_map/psum | solution.py:24
  222.5 0.1 copy.12
  222.6 0.1 copy.14
  222.7 5.8 %cholesky.55 = f32[64,64]{1,0:T(8,128)S(1)} custom-call(f32[64,64]{1,0:T(8,128)S(1)} %get-tuple-element.12), custom_call_target="Cholesky" | custom-call | tf_op jit(solution)/shard_map/jit(cholesky)/cholesky | solution.py:25
  228.6 0.6 compare_reduce_fusion
  229.2 0.7 fusion.9
  229.9 4.9 custom-call.7
  234.8 0.8 fusion.10
  235.6 5.8 %cholesky.44 = f32[64,64]{1,0:T(8,128)S(1)} custom-call(f32[64,64]{1,0:T(8,128)S(1)} %get-tuple-element.13), custom_call_target="Cholesky" | custom-call | tf_op jit(solution)/shard_map/jit(cholesky)/cholesky | solution.py:25
  241.5 0.6 compare_reduce_fusion.1
  242.2 0.7 fusion.8
  242.8 4.9 custom-call.6
  247.7 0.0 copy-done.1
  247.7 0.8 fusion.13
  248.6 5.3 %fusion.5 = f32[192,64]{0,1:T(8,128)} fusion(f32[64,3072]{1,0:T(8,128)S(1)} %fusion.13, f32[1,192,3072]{2,1,0:T(8,128)} %param.12, bf16[1,192,3072]{2,1,0:T(8,128)(2,1)} %param.10, f32[]{:T(128)S(6)} %copy.21), kind=kOutput, calls=%fused_computation.9 | convolution fusion | flops 454754304 | bytes 4374532 | tf_op jit(solution)/shard_map/dot_general | solution.py:8
  253.9 3.1 fusion.2
  257.0 0.0 all-reduce.6.cloned.1.call-update
  257.0 243.7 %all-reduce.6.cloned.1.call-done = (f32[192,64]{0,1:T(8,128)}, f32[192,64]{0,1:T(8,128)}) async-done(((f32[192,64]{0,1:T(8,128)}, f32[192,64]{0,1:T(8,128)}), (f32[192,64]{0,1:T(8,128)}, f32[192,64]{0,1:T(8,128)})) %all-reduce.6.cloned.1.call-update) | async-done | bytes 98320 | tf_op jit(solution)/shard_map/psum | solution.py:30
  500.7 0.8 broadcast_multiply_fusion.1
  501.5 0.9 broadcast_multiply_fusion
  502.4 5.8 %fusion = f32[1,192,3072]{2,1,0:T(8,128)} fusion(f32[192,64]{0,1:T(8,128)S(1)} %broadcast_multiply_fusion, f32[64,3072]{1,0:T(8,128)S(1)} %fusion.10, f32[1,192,3072]{2,1,0:T(8,128)} %param.13, f32[]{:T(128)S(6)} %copy.21, bf16[1,192,3072]{2,1,0:T(8,128)(2,1)} %param.11), kind=kOutput, calls=%fused_computation.1 | convolution fusion | flops 455344128 | bytes 6733828 | tf_op jit(solution)/shard_map/dot_general | solution.py:8
  508.2 3.7 fusion.1
  (24 shorter events, 0.1 us)
Async XLA Ops:
  7.2 0.8 copy-start
  7.2 198.3 %all-reduce.8.cloned.1.call-start = ((), (), s32[]{:S(2)}) async-start(), calls=%async_computation.1 | async-start | bytes 3145728 | tf_op jit(solution)/shard_map/psum | solution.py:23
  8.0 4.9 copy-start.5
  8.0 4.9 copy-start.8
  8.0 4.9 copy-start.11
  15.7 485.0 %all-reduce.6.cloned.1.call-start = ((), (), s32[]{:S(2)}) async-start(), calls=%async_computation | async-start | bytes 262144 | tf_op jit(solution)/shard_map/psum | solution.py:30
  205.5 2.3 copy-start.2
  205.5 42.2 %copy-start.1 = (f32[64,3072]{1,0:T(8,128)S(1)}, f32[64,3072]{1,0:T(8,128)}, u32[]{:S(2)}) copy-start(f32[64,3072]{1,0:T(8,128)} %get-tuple-element.8) | copy-start | bytes 2359300
  248.6 5.3 %copy-start.6 = (f32[1,192,3072]{2,1,0:T(8,128)S(1)}, f32[1,192,3072]{2,1,0:T(8,128)}, u32[]{:S(2)}) copy-start(f32[1,192,3072]{2,1,0:T(8,128)} %param.13) | copy-start | bytes 7077892
  248.6 5.3 %copy-start.9 = (bf16[1,192,3072]{2,1,0:T(8,128)(2,1)S(1)}, bf16[1,192,3072]{2,1,0:T(8,128)(2,1)}, u32[]{:S(2)}) copy-start(bf16[1,192,3072]{2,1,0:T(8,128)(2,1)} %param.11) | copy-start | bytes 3538948
  501.5 6.7 %copy-start.3 = (f32[192,64]{0,1:T(8,128)}, f32[192,64]{0,1:T(8,128)S(1)}, u32[]{:S(2)}) copy-start(f32[192,64]{0,1:T(8,128)S(1)} %broadcast_multiply_fusion.1) | copy-start | bytes 147460
  502.4 5.8 %copy-start.4 = (f32[192,64]{0,1:T(8,128)}, f32[192,64]{0,1:T(8,128)S(1)}, u32[]{:S(2)}) copy-start(f32[192,64]{0,1:T(8,128)S(1)} %broadcast_multiply_fusion) | copy-start | bytes 147460
  502.4 5.8 %copy-start.7 = (f32[1,192,3072]{2,1,0:T(8,128)S(1)}, f32[1,192,3072]{2,1,0:T(8,128)}, u32[]{:S(2)}) copy-start(f32[1,192,3072]{2,1,0:T(8,128)} %param.12) | copy-start | bytes 7077892
  502.4 5.8 %copy-start.10 = (bf16[1,192,3072]{2,1,0:T(8,128)(2,1)S(1)}, bf16[1,192,3072]{2,1,0:T(8,128)(2,1)}, u32[]{:S(2)}) copy-start(bf16[1,192,3072]{2,1,0:T(8,128)(2,1)} %param.10) | copy-start | bytes 3538948
Sparse Core Ops, SparseCore 0:
  15.8 189.6 all-reduce.7
  257.1 243.5 all-reduce.5
where the time goes:
time: 519 us
  waiting for transfers between devices  433 us (83%)
  matrix products  30.2 us (6%)
  other arithmetic  25.9 us (5%)
  between operations  14.8 us (3%)
  blocking collectives  14 us (3%)
    psum x1, waiting for transfers between devices, finish(): lax.psum(contract(gradient_plus_residual, orthonormal_factor, 1, 1), ('dp...  244 us
    psum x1, waiting for transfers between devices, orthonormal(): reduced_product = lax.psum(left_product, 'dp')  190 us
    dot_general x8, matrix products, contract(): lax.dot_general(left_side, right_factor, (((dims_left,), (dims_right,)),...  28.5 us
    psum x1, blocking collectives, orthonormal(): lax.psum(contract(reduced_product, reduced_product, 1, 1), 'mp')  14 us
    another operation x6, other arithmetic, orthonormal(): factor_low = jnp.linalg.cholesky(gram_matrix)  13 us
    another operation x4, other arithmetic, orthonormal(): lax.linalg.triangular_solve(factor_low, reduced_product, left_side=True,...  11.1 us
  transfers between devices with their start and end apart: 2, of which 2 were waited for; matrix products, arithmetic and copies ran while one was open for 0% of the time, Pallas kernels for 0%

commit v1 on v0

v1 whole, which is shorter than its diff:
```python
import functools
import itertools

import jax
import jax.numpy as jnp
from jax import lax
from jax.experimental import pallas as pl
from jax.experimental.pallas import tpu as pltpu
from jax.sharding import PartitionSpec as P

F32 = jnp.float32
BF16 = jnp.bfloat16
MESH = pl.DeviceIdType.MESH
NX = 4
CORES = 2


def halves(value):
    high = value.astype(BF16)
    return high, (value - high.astype(F32)).astype(BF16)


def dot(a, b, dim_a, dim_b):
    return lax.dot_general(
        a, b, (((dim_a,), (dim_b,)), ((), ())), preferred_element_type=F32
    )


def reciprocal_of(scale_ref):
    return 1.0 / jnp.full((1, 128), scale_ref[0, 0], F32)


def reduce_kernel(
    sizes,
    grad_in,
    grad_out,
    error_in,
    error_out,
    warm_in,
    warm_out,
    scale_ref,
    left_out,
    prod_out,
    inv_out,
    grads,
    errors,
    high,
    low,
    left,
    from_core,
    from_x,
    from_diag,
    from_z,
    full,
    gram,
    gram_all,
    prod,
    prod_rs,
    prod_x,
    prod_z,
    prod_full,
    elim,
    send_sems,
    recv_sems,
    load_sems,
    store_sems,
):
    ny, nz = sizes
    rows, cols = grads.shape[1:]
    rank = left.shape[1]
    half_rank = rank // CORES
    group = half_rank // NX
    half = cols // 2
    part = cols // nz
    owners = ny * CORES
    share = rows // owners

    dp = lax.axis_index("dp")
    y = lax.axis_index("mp")
    core = dp % CORES
    z = (dp // CORES) % nz
    x = dp // (CORES * nz)
    x1 = x + 1 - 2 * (x % 2)
    x3 = 3 - x
    x2 = (x + 2) % NX

    def at(x_=x, z_=z, core_=core, y_=y):
        return ((x_ * nz + z_) * CORES + core_, y_)

    owner = y * CORES + core

    def owner_at(k):
        o = (owner + k) % owners
        return o, at(core_=o % CORES, y_=o // CORES)

    loads = {}
    for m, (g, e) in enumerate(((grad_in, error_in), (grad_out, error_out))):
        for h in range(2):
            c = pl.ds(h * half, half)
            for a, (src, dst) in enumerate(((g, grads), (e, errors))):
                copy = pltpu.make_async_copy(
                    src.at[:, c], dst.at[m, :, c], load_sems.at[m, h, a]
                )
                copy.start()
                loads[m, h, a] = copy

    peers = [at(x_=(x + k) % NX) for k in range(1, NX)]
    peers += [at(z_=(z + k) % nz) for k in range(1, nz)]
    peers += [owner_at(k)[1] for k in range(1, owners)]
    barrier = pltpu.get_barrier_semaphore()
    for peer in peers:
        pl.semaphore_signal(barrier, inc=1, device_id=peer, device_id_type=MESH)

    number = itertools.count()
    sent = []

    def send(src, dst, device):
        n = next(number)
        copy = pltpu.make_async_remote_copy(
            src_ref=src,
            dst_ref=dst,
            send_sem=send_sems.at[n],
            recv_sem=recv_sems.at[n],
            device_id=device,
            device_id_type=MESH,
        )
        copy.start()
        sent.append(copy)
        return copy

    scale = reciprocal_of(scale_ref)[:, :1]

    def group_rows(g):
        return pl.ds(pl.multiple_of(core * half_rank + g * group, group), group)

    my_rows = pl.ds(pl.multiple_of(core * half_rank, half_rank), half_rank)
    other_rows = pl.ds(
        pl.multiple_of((1 - core) * half_rank, half_rank), half_rank
    )
    side = (pl.ds(0, half), pl.ds(half, half))

    def part_cols(z_):
        return pl.ds(pl.multiple_of(z_ * part, part), part)

    tile = min(512, half)
    depth = min(1024, cols)
    totals = [None, None]

    def stream(m):
        warm_high, warm_low = halves((warm_in, warm_out)[m][...])
        warm_both = jnp.concatenate([warm_high, warm_low], axis=1)
        exchanged = []
        for h in range(2):
            loads[m, h, 0].wait()
            loads[m, h, 1].wait()

            def make(t, carry, h=h):
                c = pl.ds(pl.multiple_of(h * half + t * tile, tile), tile)
                field = grads[m, :, c].astype(F32) * scale + errors[m, :, c]
                field_high, field_low = halves(field)
                high[m, 0:rows, c] = field_high
                low[m, 0:rows, c] = field_low
                both = dot(warm_both, field_high, 0, 0)
                left[m, :, c] = (
                    both[:rank]
                    + both[rank:]
                    + dot(warm_high, field_low, 0, 0)
                )
                return carry

            lax.fori_loop(0, half // tile, make, 0)
            if m == 0 and h == 0:
                pl.semaphore_wait(barrier, len(peers))
            exchanged.append(
                send(
                    left.at[m, other_rows, side[h]],
                    from_core.at[m, :, side[h]],
                    at(core_=1 - core),
                )
            )
        yield
        for h in range(2):
            exchanged[h].wait_recv()
            left[m, my_rows, side[h]] += from_core[m, :, side[h]]
        diag = [
            send(
                left.at[m, group_rows(x2), side[h]],
                from_diag.at[m, :, side[h]],
                at(x_=(x1, x3)[h]),
            )
            for h in range(2)
        ]
        near = [
            send(
                left.at[m, group_rows((x1, x3)[h]), side[h]],
                from_x.at[m, h, :, side[h]],
                at(x_=(x1, x3)[h]),
            )
            for h in range(2)
        ]
        yield
        for h in range(2):
            diag[h].wait_recv()
            g = group_rows((x3, x1)[h])
            left[m, g, side[h]] += from_diag[m, :, side[h]]
            near.append(
                send(
                    left.at[m, g, side[h]],
                    from_x.at[m, 1 - h, :, side[h]],
                    at(x_=(x3, x1)[h]),
                )
            )
        yield
        for copy in near:
            copy.wait_recv()
        mine = group_rows(x)
        left[m, mine, :] += from_x[m, 0] + from_x[m, 1]
        summed = [
            send(
                left.at[m, mine, part_cols((z + k) % nz)],
                from_z.at[m, k],
                at(z_=(z + k) % nz),
            )
            for k in range(1, nz)
        ]
        yield
        total = left[m, mine, part_cols(z)]
        for k in range(1, nz):
            summed[k - 1].wait_recv()
            total += from_z[m, k]
        full[m, mine, part_cols(z)] = total
        here = full.at[m, mine, part_cols(z)]
        spread = [send(here, here, at(z_=(z + k) % nz)) for k in range(1, nz)]
        yield
        for copy in spread:
            copy.wait_recv()
        gathered = {}
        for first in (0, 1):
            for n in range(2):
                h = 1 - n if first == 0 else n
                here = full.at[m, mine, side[h]]
                gathered[n, h] = send(here, here, at(x_=(x1, x3)[n]))
        yield
        for n in range(2):
            h = 1 - n
            gathered[n, h].wait_recv()
            here = full.at[m, group_rows((x1, x3)[n]), side[h]]
            gathered[2, h] = send(here, here, at(x_=(x3, x1)[n]))
        yield
        for n, h in ((0, 0), (1, 1), (2, 0), (2, 1)):
            gathered[n, h].wait_recv()
        here = full.at[m, my_rows, :]
        last = send(here, here, at(core_=1 - core))
        yield
        last.wait_recv()
        store = pltpu.make_async_copy(
            full.at[m], left_out.at[m], store_sems.at[m]
        )
        store.start()
        value_high, value_low = halves(full[m])
        high[m, rows : rows + rank, :] = value_high
        low[m, rows : rows + rank, :] = value_low
        total = jnp.zeros((rows + rank, 2 * rank), F32)
        for t in range(cols // depth):
            c = pl.ds(t * depth, depth)
            left_high = high[m, rows : rows + rank, c]
            left_low = low[m, rows : rows + rank, c]
            one = dot(
                high[m, :, c],
                jnp.concatenate([left_high, left_low], axis=0),
                1,
                1,
            )
            two = dot(
                low[m, :, c],
                jnp.concatenate([left_high, left_high], axis=0),
                1,
                1,
            )
            total += one + pltpu.roll(one, rank, 1) + two
        totals[m] = total
        store.wait()

    streams = [stream(0), stream(1)]
    while streams:
        for s in list(streams):
            try:
                next(s)
            except StopIteration:
                streams.remove(s)

    lane = lax.broadcasted_iota(jnp.int32, (1, 2 * rank), 1)
    packed = jnp.where(lane < rank, totals[0], totals[1])
    gram[...] = packed[rows:]
    gram_all[y] = packed[rows:]
    prod[...] = packed[:rows]
    gram_copies = [
        send(gram, gram_all.at[y], at(y_=(y + k) % ny)) for k in range(1, ny)
    ]

    def share_rows(o):
        return pl.ds(pl.multiple_of(o * share, share), share)

    rs_copies = []
    for k in range(1, owners):
        o, device = owner_at(k)
        rs_copies.append(send(prod.at[share_rows(o), :], prod_rs.at[k], device))

    for copy in gram_copies:
        copy.wait_recv()
    gram_sum = gram_all[0]
    for k in range(1, ny):
        gram_sum += gram_all[k]

    row = lax.broadcasted_iota(jnp.int32, (rank, 2 * rank), 0)
    col = lax.broadcasted_iota(jnp.int32, (rank, 2 * rank), 1)
    unit = jnp.where(col - rank == row, 1.0, 0.0).astype(F32)
    elim[0] = jnp.where(col < rank, gram_sum, unit)
    elim[1] = jnp.where(col < rank, pltpu.roll(gram_sum, rank, 1), unit)

    def step(k, carry):
        for m in range(2):
            value = elim[m]
            pivot_row = elim[m, pl.ds(k, 1), :]
            pick = col == k
            pivot_col = jnp.sum(
                jnp.where(pick, value, 0.0), axis=1, keepdims=True
            )
            pivot = jnp.sum(
                jnp.where(lane == k, pivot_row, 0.0), axis=1, keepdims=True
            )
            factor = jnp.where(row[:, :1] > k, pivot_col / pivot, 0.0)
            elim[m] = value - factor * pivot_row
        return carry

    cuts = [0, rank // 3, 2 * rank // 3, rank]

    def eliminate(n):
        lax.fori_loop(cuts[n], cuts[n + 1], step, 0)

    eliminate(0)
    total = prod[share_rows(owner), :]
    for k in range(1, owners):
        rs_copies[k - 1].wait_recv()
        total += prod_rs[k]
    prod_x[x] = total
    copies = [
        send(prod_x.at[x], prod_x.at[x], at(x_=(x + k) % NX))
        for k in range(1, NX)
    ]
    eliminate(1)
    for copy in copies:
        copy.wait_recv()
    total = prod_x[0]
    for k in range(1, NX):
        total += prod_x[k]
    prod_z[z] = total
    copies = [
        send(prod_z.at[z], prod_z.at[z], at(z_=(z + k) % nz))
        for k in range(1, nz)
    ]
    eliminate(2)
    for copy in copies:
        copy.wait_recv()
    total = prod_z[0]
    for k in range(1, nz):
        total += prod_z[k]
    prod_full[share_rows(owner), :] = total
    here = prod_full.at[share_rows(owner), :]
    copies = [send(here, here, owner_at(k)[1]) for k in range(1, owners)]

    scaled = []
    for m in range(2):
        value = elim[m]
        pivots = jnp.sum(
            jnp.where(row == col, value, 0.0), axis=1, keepdims=True
        )
        scaled.append(value / jnp.sqrt(pivots))
    inv_out[...] = jnp.where(
        lane < rank, pltpu.roll(scaled[0], rank, 1), scaled[1]
    )
    for copy in copies:
        copy.wait_recv()
    prod_out[...] = prod_full[...]
    for copy in sent:
        copy.wait_send()


def reduce_call(
    sizes, grad_in, grad_out, error_in, error_out, warm_in, warm_out, scale
):
    ny, nz = sizes
    rows, cols = grad_in.shape
    rank = warm_in.shape[1]
    half_rank = rank // CORES
    group = half_rank // NX
    owners = ny * CORES
    share = rows // owners
    any_spec = pl.BlockSpec(memory_space=pl.ANY)
    vmem = pl.BlockSpec(memory_space=pltpu.VMEM)
    smem = pl.BlockSpec(memory_space=pltpu.SMEM)
    count = 2 * (2 + 6 + 2 * (nz - 1) + 6 + 1)
    count += (ny - 1) + 2 * (owners - 1) + (NX - 1) + (nz - 1)
    return pl.pallas_call(
        functools.partial(reduce_kernel, sizes),
        out_shape=(
            jax.ShapeDtypeStruct((2, rank, cols), F32),
            jax.ShapeDtypeStruct((rows, 2 * rank), F32),
            jax.ShapeDtypeStruct((rank, 2 * rank), F32),
        ),
        in_specs=[any_spec] * 4 + [vmem, vmem, smem],
        out_specs=(any_spec, vmem, vmem),
        scratch_shapes=[
            pltpu.VMEM((2, rows, cols), BF16),
            pltpu.VMEM((2, rows, cols), F32),
            pltpu.VMEM((2, rows + rank, cols), BF16),
            pltpu.VMEM((2, rows + rank, cols), BF16),
            pltpu.VMEM((2, rank, cols), F32),
            pltpu.VMEM((2, half_rank, cols), F32),
            pltpu.VMEM((2, 2, group, cols), F32),
            pltpu.VMEM((2, group, cols), F32),
            pltpu.VMEM((2, nz, group, cols // nz), F32),
            pltpu.VMEM((2, rank, cols), F32),
            pltpu.VMEM((rank, 2 * rank), F32),
            pltpu.VMEM((ny, rank, 2 * rank), F32),
            pltpu.VMEM((rows, 2 * rank), F32),
            pltpu.VMEM((owners, share, 2 * rank), F32),
            pltpu.VMEM((NX, share, 2 * rank), F32),
            pltpu.VMEM((nz, share, 2 * rank), F32),
            pltpu.VMEM((rows, 2 * rank), F32),
            pltpu.VMEM((2, rank, 2 * rank), F32),
            pltpu.SemaphoreType.DMA((count,)),
            pltpu.SemaphoreType.DMA((count,)),
            pltpu.SemaphoreType.DMA((2, 2, 2)),
            pltpu.SemaphoreType.DMA((2,)),
        ],
        compiler_params=pltpu.CompilerParams(
            collective_id=0,
            has_side_effects=True,
            vmem_limit_bytes=40 * 1024 * 1024,
        ),
        name="reduce_left",
    )(grad_in, grad_out, error_in, error_out, warm_in, warm_out, scale)


def finish_kernel(
    replicas,
    grad_in,
    grad_out,
    error_in,
    error_out,
    left,
    prod,
    inv,
    scale_ref,
    new_error_in,
    new_error_out,
    new_warm_in,
    new_warm_out,
    factor,
):
    rank = left.shape[1]

    @pl.when(pl.program_id(0) == 0)
    def _():
        for m, out in enumerate((new_warm_in, new_warm_out)):
            lanes = slice(m * rank, (m + 1) * rank)
            inverse = inv[:, lanes]
            warm = (
                lax.dot_general(
                    prod[:, lanes],
                    inverse,
                    (((1,), (1,)), ((), ())),
                    precision=lax.Precision.HIGHEST,
                    preferred_element_type=F32,
                )
                / replicas
            )
            out[...] = warm
            applied = lax.dot_general(
                warm,
                inverse,
                (((1,), (0,)), ((), ())),
                precision=lax.Precision.HIGHEST,
                preferred_element_type=F32,
            )
            applied_high, applied_low = halves(applied)
            factor[m] = jnp.concatenate(
                [applied_high, applied_high, applied_low], axis=1
            )

    scale = reciprocal_of(scale_ref)[:, :1]
    for m, (g, e, out) in enumerate(
        ((grad_in, error_in, new_error_in), (grad_out, error_out, new_error_out))
    ):
        left_high, left_low = halves(left[m])
        stacked = jnp.concatenate([left_high, left_low, left_high], axis=0)
        field = g[...].astype(F32) * scale + e[...]
        out[...] = field - dot(factor[m], stacked, 1, 0)


def finish_call(
    replicas, grad_in, grad_out, error_in, error_out, left, prod, inv, scale
):
    rows, cols = grad_in.shape
    rank = left.shape[1]
    tile = min(512, cols)
    wide = pl.BlockSpec((rows, tile), lambda t: (0, t))
    vmem = pl.BlockSpec(memory_space=pltpu.VMEM)
    smem = pl.BlockSpec(memory_space=pltpu.SMEM)
    whole = pl.BlockSpec((rows, rank), lambda t: (0, 0))
    return pl.pallas_call(
        functools.partial(finish_kernel, replicas),
        grid=(cols // tile,),
        out_shape=(
            jax.ShapeDtypeStruct((rows, cols), F32),
            jax.ShapeDtypeStruct((rows, cols), F32),
            jax.ShapeDtypeStruct((rows, rank), F32),
            jax.ShapeDtypeStruct((rows, rank), F32),
        ),
        in_specs=[wide] * 4
        + [pl.BlockSpec((2, rank, tile), lambda t: (0, 0, t)), vmem, vmem, smem],
        out_specs=(wide, wide, whole, whole),
        scratch_shapes=[pltpu.VMEM((2, rows, 3 * rank), BF16)],
        compiler_params=pltpu.CompilerParams(
            vmem_limit_bytes=32 * 1024 * 1024,
        ),
        name="new_errors",
    )(grad_in, grad_out, error_in, error_out, left, prod, inv, scale)


def per_device(
    sizes, replicas, grad_in, grad_out, error_in, error_out, warm_in, warm_out, loss_scale
):
    wide = [a[0] for a in (grad_in, grad_out, error_in, error_out)]
    scale = loss_scale.reshape(1, 1)
    left, prod, inv = reduce_call(sizes, *wide, warm_in, warm_out, scale)
    err_in, err_out, new_in, new_out = finish_call(
        replicas, *wide, left, prod, inv, scale
    )
    return err_in[None], err_out[None], new_in, new_out


def solution(mesh):
    wide = P("dp", None, "mp")
    sizes = (mesh.shape["mp"], mesh.shape["dp"] // (NX * CORES))
    return jax.shard_map(
        functools.partial(per_device, sizes, float(mesh.shape["dp"])),
        mesh=mesh,
        in_specs=(wide, wide, wide, wide, P(), P(), P()),
        out_specs=(wide, wide, P(), P()),
        check_vma=False,
    )
```

time: 519 us -> 81.9 us (0.16)
  waiting for transfers between devices: 433 us -> 0 us
  Pallas kernels: 0 us -> 71.1 us
  matrix products: 30.2 us -> 0 us
  other arithmetic: 25.9 us -> 0 us
  blocking collectives: 14 us -> 0 us
  between operations: 14.8 us -> 1.31 us
  local copies, waits for them, and re-layouts: 0.36 us -> 9.17 us
    psum x2 -> x0, waiting for transfers between devices: 433 us -> none  [the longest x1 244 us: finish(): lax.psum(contract(gradient_plus_residual, orthonormal_factor, 1, 1), ('dp...]
    pallas_call x0 -> x2, Pallas kernels: none -> 71.1 us  [the longest x1 66.1 us: reduce_call(): pl.pallas_call(functools.partial(reduce_kernel, sizes), out_shape=(jax.Sh...]
    dot_general x8 -> x0, matrix products: 28.5 us -> none  [contract(): lax.dot_general(left_side, right_factor, (((dims_left,), (dims_right,)),...]
    another operation x10 -> x0, other arithmetic: 24.1 us -> none  [the longest x6 13 us: orthonormal(): factor_low = jnp.linalg.cholesky(gram_matrix)]
    psum x1 -> x0, blocking collectives: 14 us -> none  [orthonormal(): lax.psum(contract(reduced_product, reduced_product, 1, 1), 'mp')]
    unnamed x24 -> x14, local copies, waits for them, and re-layouts: 0.21 us -> 9.17 us
  transfers between devices with their start and end apart: 2 -> 0, of which waited for: 2 -> 0; matrix products, arithmetic and copies ran while one was open for 0% -> 0% of each run, Pallas kernels for 0% -> 0%
where the time goes in v1:
time: 81.9 us; the launch traced here: 81.6 us
  Pallas kernels  71.1 us (87%)
  local copies, waits for them, and re-layouts  9.17 us (11%)
  between operations  1.31 us (2%)
    pallas_call x1, Pallas kernels, reduce_call(): pl.pallas_call(functools.partial(reduce_kernel, sizes), out_shape=(jax.Sh...  66.1 us
    unnamed x14, local copies, waits for them, and re-layouts  9.17 us
    pallas_call x1, Pallas kernels, finish_call(): pl.pallas_call(functools.partial(finish_kernel, replicas), grid=(cols //...  5.06 us

profile of v1, /device:TPU:1, one launch (start us, length us, event | category | flops | bytes accessed | tf_op | source)
XLA Modules:
  0.0 81.6 jit_solution(4875630810691510582)
XLA Ops:
  1.3 0.9 %copy.11.warm_in = f32[192,64]{1,0:T(8,128)S(1)} copy(f32[192,64]{0,1:T(8,128)} %param.11) | data formatting | bytes 98304 | tf_op args[4]
  2.2 0.9 %copy.12.warm_out = f32[192,64]{1,0:T(8,128)S(1)} copy(f32[192,64]{0,1:T(8,128)} %param.12) | data formatting | bytes 98304 | tf_op args[5]
  3.2 0.0 copy-start
  3.2 1.7 %copy-done = f32[1,192,3072]{2,1,0:T(8,128)S(1)} copy-done((f32[1,192,3072]{2,1,0:T(8,128)S(1)}, f32[1,192,3072]{2,1,0:T(8,128)}, u32[]{:S(2)}) %copy-start) | copy-done | bytes 2359320
  4.8 0.0 copy-start.1
  4.8 1.7 %copy-done.1 = f32[1,192,3072]{2,1,0:T(8,128)S(1)} copy-done((f32[1,192,3072]{2,1,0:T(8,128)S(1)}, f32[1,192,3072]{2,1,0:T(8,128)}, u32[]{:S(2)}) %copy-start.1) | copy-done | bytes 2359320
  6.5 0.0 copy-start.2
  6.5 1.3 %copy-done.2 = bf16[1,192,3072]{2,1,0:T(8,128)(2,1)S(1)} copy-done((bf16[1,192,3072]{2,1,0:T(8,128)(2,1)S(1)}, bf16[1,192,3072]{2,1,0:T(8,128)(2,1)}, u32[]{:S(2)}) %copy-start.2) | copy-done | bytes 1179672
  7.8 0.0 copy-start.4
  7.8 1.3 %copy-done.4 = bf16[1,192,3072]{2,1,0:T(8,128)(2,1)S(1)} copy-done((bf16[1,192,3072]{2,1,0:T(8,128)(2,1)S(1)}, bf16[1,192,3072]{2,1,0:T(8,128)(2,1)}, u32[]{:S(2)}) %copy-start.4) | copy-done | bytes 1179672
  9.0 0.0 copy-start.3
  9.0 66.1 %reduce_left.1 = (f32[2,64,3072]{2,1,0:T(8,128)S(1)}, f32[192,128]{1,0:T(8,128)S(1)}, f32[64,128]{1,0:T(8,128)S(1)}) custom-call(bf16[192,3072]{1,0:T(8,128)(2,1)S(1)} %bitcast.13, bf16[192,3072]{1,0:T(8,128)(2,1)S(1)} %bitcast.15, f32[192,3072]{1,0:T(8,128)S(1)} %bitcast.9, f32[192,3072]{1,0:T(8,128)S(1)} %bitcast.11, f32[192,64]{1,0:T(8,128)S(1)} %copy.11.warm_in, ...), custom_call_target="tpu_custom_call" | custom-call | tf_op jit(solution)/shard_map/reduce_left/pallas_call | solution.py:404
  75.1 0.0 copy-done.3
  75.1 5.1 %new_errors.1 = (f32[192,3072]{1,0:T(8,128)}, f32[192,3072]{1,0:T(8,128)}, f32[192,64]{1,0:T(8,128)S(1)}, f32[192,64]{1,0:T(8,128)S(1)}) custom-call(bf16[192,3072]{1,0:T(8,128)(2,1)S(1)} %bitcast.14, bf16[192,3072]{1,0:T(8,128)(2,1)S(1)} %bitcast.16, f32[192,3072]{1,0:T(8,128)S(1)} %bitcast.10, f32[192,3072]{1,0:T(8,128)S(1)} %bitcast.12, ...), custom_call_target="tpu_custom_call" | custom-call | tf_op jit(solution)/shard_map/new_errors/pallas_call | solution.py:512
  80.2 0.7 copy.13
  80.9 0.7 copy.14
Async XLA Ops:
  3.2 1.7 %copy-start = (f32[1,192,3072]{2,1,0:T(8,128)S(1)}, f32[1,192,3072]{2,1,0:T(8,128)}, u32[]{:S(2)}) copy-start(f32[1,192,3072]{2,1,0:T(8,128)} %param.9) | copy-start | bytes 7077892
  4.8 1.7 %copy-start.1 = (f32[1,192,3072]{2,1,0:T(8,128)S(1)}, f32[1,192,3072]{2,1,0:T(8,128)}, u32[]{:S(2)}) copy-start(f32[1,192,3072]{2,1,0:T(8,128)} %param.10) | copy-start | bytes 7077892
  6.5 1.3 %copy-start.2 = (bf16[1,192,3072]{2,1,0:T(8,128)(2,1)S(1)}, bf16[1,192,3072]{2,1,0:T(8,128)(2,1)}, u32[]{:S(2)}) copy-start(bf16[1,192,3072]{2,1,0:T(8,128)(2,1)} %param.7) | copy-start | bytes 3538948
  7.8 1.3 %copy-start.4 = (bf16[1,192,3072]{2,1,0:T(8,128)(2,1)S(1)}, bf16[1,192,3072]{2,1,0:T(8,128)(2,1)}, u32[]{:S(2)}) copy-start(bf16[1,192,3072]{2,1,0:T(8,128)(2,1)} %param.8) | copy-start | bytes 3538948
  9.0 66.1 %copy-start.3 = (bf16[1,192,3072]{2,1,0:T(8,128)(2,1)S(1)}, bf16[1,192,3072]{2,1,0:T(8,128)(2,1)}, u32[]{:S(2)}) copy-start(bf16[1,192,3072]{2,1,0:T(8,128)(2,1)} %param.7) | copy-start | bytes 3538948

commit v2 on v1

--- a/solution.py
+++ b/solution.py
@@ -39,11 +39,13 @@
     warm_in,
     warm_out,
     scale_ref,
+    fields,
     left_out,
     prod_out,
     inv_out,
     grads,
     errors,
+    warms,
     high,
     low,
     left,
@@ -63,7 +65,7 @@
     send_sems,
     recv_sems,
     load_sems,
-    store_sems,
+    warm_sems,
 ):
     ny, nz = sizes
     rows, cols = grads.shape[1:]
@@ -103,6 +105,10 @@
                 )
                 copy.start()
                 loads[m, h, a] = copy
+
+    for m, w in enumerate((warm_in, warm_out)):
+        loads[m, "w"] = pltpu.make_async_copy(w, warms.at[m], warm_sems.at[m])
+        loads[m, "w"].start()
 
     peers = [at(x_=(x + k) % NX) for k in range(1, NX)]
     peers += [at(z_=(z + k) % nz) for k in range(1, nz)]
@@ -147,8 +153,9 @@
     totals = [None, None]
 
     def stream(m):
-        warm_high, warm_low = halves((warm_in, warm_out)[m][...])
-        warm_both = jnp.concatenate([warm_high, warm_low], axis=1)
+        loads[m, "w"].wait()
+        warm_high, warm_low = halves(warms[m])
+        warm_both = jnp.concatenate([warm_high, warm_low], axis=0)
         exchanged = []
         for h in range(2):
             loads[m, h, 0].wait()
@@ -158,13 +165,14 @@
                 c = pl.ds(pl.multiple_of(h * half + t * tile, tile), tile)
                 field = grads[m, :, c].astype(F32) * scale + errors[m, :, c]
                 field_high, field_low = halves(field)
+                fields[m, :, c] = field
                 high[m, 0:rows, c] = field_high
                 low[m, 0:rows, c] = field_low
-                both = dot(warm_both, field_high, 0, 0)
+                both = dot(warm_both, field_high, 1, 0)
                 left[m, :, c] = (
                     both[:rank]
                     + both[rank:]
-                    + dot(warm_high, field_low, 0, 0)
+                    + dot(warm_high, field_low, 1, 0)
                 )
                 return carry
 
@@ -178,27 +186,27 @@
                     at(core_=1 - core),
                 )
             )
-        yield
+            yield
+        diag, near = [], []
         for h in range(2):
             exchanged[h].wait_recv()
             left[m, my_rows, side[h]] += from_core[m, :, side[h]]
-        diag = [
-            send(
-                left.at[m, group_rows(x2), side[h]],
-                from_diag.at[m, :, side[h]],
-                at(x_=(x1, x3)[h]),
-            )
-            for h in range(2)
-        ]
-        near = [
-            send(
-                left.at[m, group_rows((x1, x3)[h]), side[h]],
-                from_x.at[m, h, :, side[h]],
-                at(x_=(x1, x3)[h]),
-            )
-            for h in range(2)
-        ]
-        yield
+            neighbour = (x1, x3)[h]
+            diag.append(
+                send(
+                    left.at[m, group_rows(x2), side[h]],
+                    from_diag.at[m, :, side[h]],
+                    at(x_=neighbour),
+                )
+            )
+            near.append(
+                send(
+                    left.at[m, group_rows(neighbour), side[h]],
+                    from_x.at[m, h, :, side[h]],
+                    at(x_=neighbour),
+                )
+            )
+            yield
         for h in range(2):
             diag[h].wait_recv()
             g = group_rows((x3, x1)[h])
@@ -240,6 +248,8 @@
                 h = 1 - n if first == 0 else n
                 here = full.at[m, mine, side[h]]
                 gathered[n, h] = send(here, here, at(x_=(x1, x3)[n]))
+        here = full.at[m, mine, :]
+        shared = [send(here, here, at(core_=1 - core))]
         yield
         for n in range(2):
             h = 1 - n
@@ -247,17 +257,20 @@
             here = full.at[m, group_rows((x1, x3)[n]), side[h]]
             gathered[2, h] = send(here, here, at(x_=(x3, x1)[n]))
         yield
-        for n, h in ((0, 0), (1, 1), (2, 0), (2, 1)):
-            gathered[n, h].wait_recv()
-        here = full.at[m, my_rows, :]
-        last = send(here, here, at(core_=1 - core))
+        for n in range(2):
+            gathered[n, n].wait_recv()
+            here = full.at[m, group_rows((x1, x3)[n]), :]
+            shared.append(send(here, here, at(core_=1 - core)))
+        for h in range(2):
+            gathered[2, h].wait_recv()
+            here = full.at[m, group_rows(x2), side[h]]
+            shared.append(send(here, here, at(core_=1 - core)))
         yield
-        last.wait_recv()
-        store = pltpu.make_async_copy(
-            full.at[m], left_out.at[m], store_sems.at[m]
-        )
-        store.start()
+        for copy in shared:
+            copy.wait_recv()
         value_high, value_low = halves(full[m])
+        left_out[m, :rank] = value_high
+        left_out[m, rank:] = value_low
         high[m, rows : rows + rank, :] = value_high
         low[m, rows : rows + rank, :] = value_low
         total = jnp.zeros((rows + rank, 2 * rank), F32)
@@ -279,15 +292,10 @@
             )
             total += one + pltpu.roll(one, rank, 1) + two
         totals[m] = total
-        store.wait()
-
-    streams = [stream(0), stream(1)]
-    while streams:
-        for s in list(streams):
-            try:
-                next(s)
-            except StopIteration:
-                streams.remove(s)
+
+    streams = (stream(0), stream(1))
+    for m in (0, 0, 1, 0, 0, 1, 1, 0, 1, 0, 1, 1, 0, 1, 0, 1, 0, 1, 0, 0, 1, 1):
+        next(streams[m], None)
 
     lane = lax.broadcasted_iota(jnp.int32, (1, 2 * rank), 1)
     packed = jnp.where(lane < rank, totals[0], totals[1])
@@ -306,39 +314,6 @@
         o, device = owner_at(k)
         rs_copies.append(send(prod.at[share_rows(o), :], prod_rs.at[k], device))
 
-    for copy in gram_copies:
-        copy.wait_recv()
-    gram_sum = gram_all[0]
-    for k in range(1, ny):
-        gram_sum += gram_all[k]
-
-    row = lax.broadcasted_iota(jnp.int32, (rank, 2 * rank), 0)
-    col = lax.broadcasted_iota(jnp.int32, (rank, 2 * rank), 1)
-    unit = jnp.where(col - rank == row, 1.0, 0.0).astype(F32)
-    elim[0] = jnp.where(col < rank, gram_sum, unit)
-    elim[1] = jnp.where(col < rank, pltpu.roll(gram_sum, rank, 1), unit)
-
-    def step(k, carry):
-        for m in range(2):
-            value = elim[m]
-            pivot_row = elim[m, pl.ds(k, 1), :]
-            pick = col == k
-            pivot_col = jnp.sum(
-                jnp.where(pick, value, 0.0), axis=1, keepdims=True
-            )
-            pivot = jnp.sum(
-                jnp.where(lane == k, pivot_row, 0.0), axis=1, keepdims=True
-            )
-            factor = jnp.where(row[:, :1] > k, pivot_col / pivot, 0.0)
-            elim[m] = value - factor * pivot_row
-        return carry
-
-    cuts = [0, rank // 3, 2 * rank // 3, rank]
-
-    def eliminate(n):
-        lax.fori_loop(cuts[n], cuts[n + 1], step, 0)
-
-    eliminate(0)
     total = prod[share_rows(owner), :]
     for k in range(1, owners):
         rs_copies[k - 1].wait_recv()
@@ -348,7 +323,40 @@
         send(prod_x.at[x], prod_x.at[x], at(x_=(x + k) % NX))
         for k in range(1, NX)
     ]
-    eliminate(1)
+
+    for copy in gram_copies:
+        copy.wait_recv()
+    gram_sum = gram_all[0]
+    for k in range(1, ny):
+        gram_sum += gram_all[k]
+
+    row = lax.broadcasted_iota(jnp.int32, (rank, 2 * rank), 0)
+    col = lax.broadcasted_iota(jnp.int32, (rank, 2 * rank), 1)
+    unit = jnp.where(col - rank == row, 1.0, 0.0).astype(F32)
+    elim[0] = jnp.where(col < rank, gram_sum, unit)
+    elim[1] = jnp.where(col < rank, pltpu.roll(gram_sum, rank, 1), unit)
+
+    def step(k, carry):
+        for m in range(2):
+            value = elim[m]
+            pivot_row = elim[m, pl.ds(k, 1), :]
+            pick = col == k
+            pivot_col = jnp.sum(
+                jnp.where(pick, value, 0.0), axis=1, keepdims=True
+            )
+            pivot = jnp.sum(
+                jnp.where(lane == k, pivot_row, 0.0), axis=1, keepdims=True
+            )
+            factor = jnp.where(row[:, :1] > k, pivot_col / pivot, 0.0)
+            elim[m] = value - factor * pivot_row
+        return carry
+
+    cuts = [0, 5 * rank // 16, 3 * rank // 4, rank]
+
+    def eliminate(n):
+        lax.fori_loop(cuts[n], cuts[n + 1], step, 0)
+
+    eliminate(0)
     for copy in copies:
         copy.wait_recv()
     total = prod_x[0]
@@ -359,7 +367,7 @@
         send(prod_z.at[z], prod_z.at[z], at(z_=(z + k) % nz))
         for k in range(1, nz)
     ]
-    eliminate(2)
+    eliminate(1)
     for copy in copies:
         copy.wait_recv()
     total = prod_z[0]
@@ -368,6 +376,7 @@
     prod_full[share_rows(owner), :] = total
     here = prod_full.at[share_rows(owner), :]
     copies = [send(here, here, owner_at(k)[1]) for k in range(1, owners)]
+    eliminate(2)
 
     scaled = []
     for m in range(2):
@@ -391,28 +400,30 @@
 ):
     ny, nz = sizes
     rows, cols = grad_in.shape
-    rank = warm_in.shape[1]
+    rank = warm_in.shape[0]
     half_rank = rank // CORES
     group = half_rank // NX
     owners = ny * CORES
     share = rows // owners
-    any_spec = pl.BlockSpec(memory_space=pl.ANY)
+    hbm = pl.BlockSpec(memory_space=pltpu.HBM)
     vmem = pl.BlockSpec(memory_space=pltpu.VMEM)
     smem = pl.BlockSpec(memory_space=pltpu.SMEM)
-    count = 2 * (2 + 6 + 2 * (nz - 1) + 6 + 1)
+    count = 2 * (2 + 6 + 2 * (nz - 1) + 6 + 5)
     count += (ny - 1) + 2 * (owners - 1) + (NX - 1) + (nz - 1)
     return pl.pallas_call(
         functools.partial(reduce_kernel, sizes),
         out_shape=(
-            jax.ShapeDtypeStruct((2, rank, cols), F32),
-            jax.ShapeDtypeStruct((rows, 2 * rank), F32),
-            jax.ShapeDtypeStruct((rank, 2 * rank), F32),
+            pltpu.VMEM((2, rows, cols), F32),
+            pltpu.VMEM((2, 2 * rank, cols), BF16),
+            pltpu.VMEM((rows, 2 * rank), F32),
+            pltpu.VMEM((rank, 2 * rank), F32),
         ),
-        in_specs=[any_spec] * 4 + [vmem, vmem, smem],
-        out_specs=(any_spec, vmem, vmem),
+        in_specs=[hbm] * 6 + [smem],
+        out_specs=(vmem,) * 4,
         scratch_shapes=[
             pltpu.VMEM((2, rows, cols), BF16),
             pltpu.VMEM((2, rows, cols), F32),
+            pltpu.VMEM((2, rank, rows), F32),
             pltpu.VMEM((2, rows + rank, cols), BF16),
             pltpu.VMEM((2, rows + rank, cols), BF16),
             pltpu.VMEM((2, rank, cols), F32),
@@ -445,100 +456,94 @@
 
 def finish_kernel(
     replicas,
-    grad_in,
-    grad_out,
-    error_in,
-    error_out,
+    fields,
     left,
     prod,
     inv,
-    scale_ref,
     new_error_in,
     new_error_out,
     new_warm_in,
     new_warm_out,
     factor,
+    made,
+    store_sems,
 ):
-    rank = left.shape[1]
-
-    @pl.when(pl.program_id(0) == 0)
-    def _():
-        for m, out in enumerate((new_warm_in, new_warm_out)):
-            lanes = slice(m * rank, (m + 1) * rank)
-            inverse = inv[:, lanes]
-            warm = (
-                lax.dot_general(
-                    prod[:, lanes],
-                    inverse,
-                    (((1,), (1,)), ((), ())),
-                    precision=lax.Precision.HIGHEST,
-                    preferred_element_type=F32,
-                )
-                / replicas
-            )
-            out[...] = warm
-            applied = lax.dot_general(
-                warm,
-                inverse,
-                (((1,), (0,)), ((), ())),
-                precision=lax.Precision.HIGHEST,
-                preferred_element_type=F32,
-            )
-            applied_high, applied_low = halves(applied)
-            factor[m] = jnp.concatenate(
-                [applied_high, applied_high, applied_low], axis=1
-            )
-
-    scale = reciprocal_of(scale_ref)[:, :1]
-    for m, (g, e, out) in enumerate(
-        ((grad_in, error_in, new_error_in), (grad_out, error_out, new_error_out))
-    ):
-        left_high, left_low = halves(left[m])
-        stacked = jnp.concatenate([left_high, left_low, left_high], axis=0)
-        field = g[...].astype(F32) * scale + e[...]
-        out[...] = field - dot(factor[m], stacked, 1, 0)
-
-
-def finish_call(
-    replicas, grad_in, grad_out, error_in, error_out, left, prod, inv, scale
-):
-    rows, cols = grad_in.shape
-    rank = left.shape[1]
+    rows, cols = fields.shape[1:]
+    rank = inv.shape[0]
+    tile = made.shape[-1]
+    exact = functools.partial(
+        lax.dot_general,
+        precision=lax.Precision.HIGHEST,
+        preferred_element_type=F32,
+    )
+    stores = []
+    for m, warm_out in enumerate((new_warm_in, new_warm_out)):
+        lanes = slice(m * rank, (m + 1) * rank)
+        inverse = inv[:, lanes]
+        warm = exact(inverse, prod[:, lanes], (((1,), (1,)), ((), ()))) / replicas
+        warm_out[...] = warm
+        applied = exact(warm, inverse, (((0,), (0,)), ((), ())))
+        applied_high, applied_low = halves(applied)
+        factor[m] = jnp.concatenate(
+            [applied_high, applied_high, applied_low], axis=1
+        )
+    for m, out in enumerate((new_error_in, new_error_out)):
+        for t in range(cols // tile):
+            c = pl.ds(t * tile, tile)
+            stacked = jnp.concatenate([left[m, :, c], left[m, :rank, c]], axis=0)
+            made[m, t] = fields[m, :, c] - dot(factor[m], stacked, 1, 0)
+            store = pltpu.make_async_copy(
+                made.at[m, t], out.at[:, c], store_sems.at[m, t]
+            )
+            store.start()
+            stores.append(store)
+    for store in stores:
+        store.wait()
+
+
+def finish_call(replicas, fields, left, prod, inv):
+    rows, cols = fields.shape[1:]
+    rank = inv.shape[0]
     tile = min(512, cols)
-    wide = pl.BlockSpec((rows, tile), lambda t: (0, t))
     vmem = pl.BlockSpec(memory_space=pltpu.VMEM)
-    smem = pl.BlockSpec(memory_space=pltpu.SMEM)
-    whole = pl.BlockSpec((rows, rank), lambda t: (0, 0))
+    hbm = pl.BlockSpec(memory_space=pltpu.HBM)
     return pl.pallas_call(
         functools.partial(finish_kernel, replicas),
-        grid=(cols // tile,),
         out_shape=(
             jax.ShapeDtypeStruct((rows, cols), F32),
             jax.ShapeDtypeStruct((rows, cols), F32),
-            jax.ShapeDtypeStruct((rows, rank), F32),
-            jax.ShapeDtypeStruct((rows, rank), F32),
+            jax.ShapeDtypeStruct((rank, rows), F32),
+            jax.ShapeDtypeStruct((rank, rows), F32),
         ),
-        in_specs=[wide] * 4
-        + [pl.BlockSpec((2, rank, tile), lambda t: (0, 0, t)), vmem, vmem, smem],
-        out_specs=(wide, wide, whole, whole),
-        scratch_shapes=[pltpu.VMEM((2, rows, 3 * rank), BF16)],
+        in_specs=[vmem] * 4,
+        out_specs=(hbm, hbm, vmem, vmem),
+        scratch_shapes=[
+            pltpu.VMEM((2, rows, 3 * rank), BF16),
+            pltpu.VMEM((2, cols // tile, rows, tile), F32),
+            pltpu.SemaphoreType.DMA((2, cols // tile)),
+        ],
         compiler_params=pltpu.CompilerParams(
             vmem_limit_bytes=32 * 1024 * 1024,
         ),
         name="new_errors",
-    )(grad_in, grad_out, error_in, error_out, left, prod, inv, scale)
+    )(fields, left, prod, inv)
 
 
 def per_device(
     sizes, replicas, grad_in, grad_out, error_in, error_out, warm_in, warm_out, loss_scale
 ):
-    wide = [a[0] for a in (grad_in, grad_out, error_in, error_out)]
+    wide = [
+        pltpu.with_memory_space_constraint(a[0], pltpu.HBM)
+        for a in (grad_in, grad_out, error_in, error_out)
+    ]
     scale = loss_scale.reshape(1, 1)
-    left, prod, inv = reduce_call(sizes, *wide, warm_in, warm_out, scale)
-    err_in, err_out, new_in, new_out = finish_call(
-        replicas, *wide, left, prod, inv, scale
-    )
-    return err_in[None], err_out[None], new_in, new_out
+    warms = [
+        pltpu.with_memory_space_constraint(a.T, pltpu.HBM)
+        for a in (warm_in, warm_out)
+    ]
+    reduced = reduce_call(sizes, *wide, *warms, scale)
+    err_in, err_out, new_in, new_out = finish_call(replicas, *reduced)
+    return err_in[None], err_out[None], new_in.T, new_out.T
 
 
 def solution(mesh):

time: 81.9 us -> 68.9 us (0.84)
  local copies, waits for them, and re-layouts: 9.17 us -> 0 us
  Pallas kernels: 71.1 us -> 67.5 us
    unnamed x14 -> x0, local copies, waits for them, and re-layouts: 9.17 us -> none
    pallas_call x2, Pallas kernels: 71.1 us -> 67.5 us  [the longest x1 63.1 us: reduce_call(): pl.pallas_call(functools.partial(reduce_kernel, sizes), out_shape=(pltpu....]
where the time goes in v2:
time: 68.9 us; the launch traced here: 68.8 us
  Pallas kernels  67.5 us (98%)
  between operations  1.29 us (2%)
    pallas_call x1, Pallas kernels, reduce_call(): pl.pallas_call(functools.partial(reduce_kernel, sizes), out_shape=(pltpu....  63.1 us
    pallas_call x1, Pallas kernels, finish_call(): pl.pallas_call(functools.partial(finish_kernel, replicas), out_shape=(jax...  4.41 us

profile of v2, /device:TPU:1, one launch (start us, length us, event | category | flops | bytes accessed | tf_op | source)
XLA Modules:
  0.0 68.8 jit_solution(2256467036345606594)
XLA Ops:
  1.3 63.1 %reduce_left.1 = (f32[2,192,3072]{2,1,0:T(8,128)S(1)}, bf16[2,128,3072]{2,1,0:T(8,128)(2,1)S(1)}, f32[192,128]{1,0:T(8,128)S(1)}, f32[64,128]{1,0:T(8,128)S(1)}) custom-call(bf16[192,3072]{1,0:T(8,128)(2,1)} %bitcast.14, bf16[192,3072]{1,0:T(8,128)(2,1)} %bitcast.15, f32[192,3072]{1,0:T(8,128)} %bitcast.12, f32[192,3072]{1,0:T(8,128)} %bitcast.13, ...), custom_call_target="tpu_custom_call" | custom-call | tf_op jit(solution)/shard_map/reduce_left/pallas_call | solution.py:413
  64.4 4.4 %new_errors.1 = (f32[192,3072]{1,0:T(8,128)}, f32[192,3072]{1,0:T(8,128)}, f32[64,192]{1,0:T(8,128)}, f32[64,192]{1,0:T(8,128)}) custom-call(f32[2,192,3072]{2,1,0:T(8,128)S(1)} %get-tuple-element.12.fields, bf16[2,128,3072]{2,1,0:T(8,128)(2,1)S(1)} %get-tuple-element.13.left, f32[192,128]{1,0:T(8,128)S(1)} %get-tuple-element.14.prod, ...), custom_call_target="tpu_custom_call" | custom-call | tf_op jit(solution)/shard_map/new_errors/pallas_call | solution.py:510

commit v3 on v2

--- a/solution.py
+++ b/solution.py
@@ -49,12 +49,15 @@
     high,
     low,
     left,
+    left_other,
+    left_core,
     from_core,
     from_x,
     from_diag,
     from_z,
     full,
     gram,
+    gram_core,
     gram_all,
     prod,
     prod_rs,
@@ -70,10 +73,12 @@
     ny, nz = sizes
     rows, cols = grads.shape[1:]
     rank = left.shape[1]
-    half_rank = rank // CORES
-    group = half_rank // NX
-    half = cols // 2
-    part = cols // nz
+    group = rank // NX
+    half = cols // CORES
+    piece = half // 2
+    part_rows = from_z.shape[2]
+    part = from_z.shape[3]
+    across = half // part
     owners = ny * CORES
     share = rows // owners
 
@@ -95,20 +100,26 @@
         o = (owner + k) % owners
         return o, at(core_=o % CORES, y_=o // CORES)
 
+    mine_at = core * half
+    other_at = (1 - core) * half
+
+    def columns(start, width):
+        return pl.ds(pl.multiple_of(start, width), width)
+
     loads = {}
-    for m, (g, e) in enumerate(((grad_in, error_in), (grad_out, error_out))):
-        for h in range(2):
-            c = pl.ds(h * half, half)
-            for a, (src, dst) in enumerate(((g, grads), (e, errors))):
-                copy = pltpu.make_async_copy(
-                    src.at[:, c], dst.at[m, :, c], load_sems.at[m, h, a]
-                )
-                copy.start()
-                loads[m, h, a] = copy
-
     for m, w in enumerate((warm_in, warm_out)):
         loads[m, "w"] = pltpu.make_async_copy(w, warms.at[m], warm_sems.at[m])
         loads[m, "w"].start()
+    for m, (g, e) in enumerate(((grad_in, error_in), (grad_out, error_out))):
+        for b, start in enumerate((other_at, mine_at)):
+            for h in range(2):
+                c = columns(start + h * piece, piece)
+                for a, (src, dst) in enumerate(((g, grads), (e, errors))):
+                    copy = pltpu.make_async_copy(
+                        src.at[:, c], dst.at[m, :, c], load_sems.at[m, b, h, a]
+                    )
+                    copy.start()
+                    loads[m, b, h, a] = copy
 
     peers = [at(x_=(x + k) % NX) for k in range(1, NX)]
     peers += [at(z_=(z + k) % nz) for k in range(1, nz)]
@@ -137,60 +148,70 @@
     scale = reciprocal_of(scale_ref)[:, :1]
 
     def group_rows(g):
-        return pl.ds(pl.multiple_of(core * half_rank + g * group, group), group)
-
-    my_rows = pl.ds(pl.multiple_of(core * half_rank, half_rank), half_rank)
-    other_rows = pl.ds(
-        pl.multiple_of((1 - core) * half_rank, half_rank), half_rank
-    )
-    side = (pl.ds(0, half), pl.ds(half, half))
-
-    def part_cols(z_):
-        return pl.ds(pl.multiple_of(z_ * part, part), part)
-
-    tile = min(512, half)
-    depth = min(1024, cols)
+        return pl.ds(pl.multiple_of(g * group, group), group)
+
+    side = (pl.ds(0, piece), pl.ds(piece, piece))
+
+    def full_side(h):
+        return columns(mine_at + h * piece, piece)
+
+    def part_rows_of(g, z_):
+        start = g * group + z_ // across * part_rows
+        return pl.ds(pl.multiple_of(start, part_rows), part_rows)
+
+    def part_cols(z_, start=0):
+        return columns(start + z_ % across * part, part)
+
+    tile = min(384, piece)
+    depth = min(768, half)
     totals = [None, None]
+    shared = []
 
     def stream(m):
+        exchanged = []
         loads[m, "w"].wait()
         warm_high, warm_low = halves(warms[m])
         warm_both = jnp.concatenate([warm_high, warm_low], axis=0)
-        exchanged = []
-        for h in range(2):
-            loads[m, h, 0].wait()
-            loads[m, h, 1].wait()
-
-            def make(t, carry, h=h):
-                c = pl.ds(pl.multiple_of(h * half + t * tile, tile), tile)
+
+        def make(b, h, out):
+            loads[m, b, h, 0].wait()
+            loads[m, b, h, 1].wait()
+            start = (other_at, mine_at)[b] + h * piece
+
+            def one(t, carry):
+                c = columns(start + t * tile, tile)
                 field = grads[m, :, c].astype(F32) * scale + errors[m, :, c]
+                fields[m, :, c] = field
                 field_high, field_low = halves(field)
-                fields[m, :, c] = field
-                high[m, 0:rows, c] = field_high
-                low[m, 0:rows, c] = field_low
                 both = dot(warm_both, field_high, 1, 0)
-                left[m, :, c] = (
+                out[m, :, columns(h * piece + t * tile, tile)] = (
                     both[:rank]
                     + both[rank:]
                     + dot(warm_high, field_low, 1, 0)
                 )
                 return carry
 
-            lax.fori_loop(0, half // tile, make, 0)
+            lax.fori_loop(0, piece // tile, one, 0)
+
+        for h in range(2):
+            make(0, h, left_other)
             if m == 0 and h == 0:
                 pl.semaphore_wait(barrier, len(peers))
             exchanged.append(
                 send(
-                    left.at[m, other_rows, side[h]],
-                    from_core.at[m, :, side[h]],
+                    left_other.at[m, :, side[h]],
+                    left_core.at[m, :, side[h]],
                     at(core_=1 - core),
                 )
             )
-            yield
+        yield
+        for h in range(2):
+            make(1, h, left)
+        yield
         diag, near = [], []
         for h in range(2):
             exchanged[h].wait_recv()
-            left[m, my_rows, side[h]] += from_core[m, :, side[h]]
+            left[m, :, side[h]] += left_core[m, :, side[h]]
             neighbour = (x1, x3)[h]
             diag.append(
                 send(
@@ -218,6 +239,11 @@
                     at(x_=(x3, x1)[h]),
                 )
             )
+        other = send(
+            fields.at[m, :, columns(other_at, half)],
+            from_core.at[m],
+            at(core_=1 - core),
+        )
         yield
         for copy in near:
             copy.wait_recv()
@@ -225,20 +251,33 @@
         left[m, mine, :] += from_x[m, 0] + from_x[m, 1]
         summed = [
             send(
-                left.at[m, mine, part_cols((z + k) % nz)],
+                left.at[m, part_rows_of(x, (z + k) % nz), part_cols((z + k) % nz)],
                 from_z.at[m, k],
                 at(z_=(z + k) % nz),
             )
             for k in range(1, nz)
         ]
         yield
-        total = left[m, mine, part_cols(z)]
+        total = left[m, part_rows_of(x, z), part_cols(z)]
         for k in range(1, nz):
             summed[k - 1].wait_recv()
             total += from_z[m, k]
-        full[m, mine, part_cols(z)] = total
-        here = full.at[m, mine, part_cols(z)]
+        full[m, part_rows_of(x, z), part_cols(z, mine_at)] = total
+        here = full.at[m, part_rows_of(x, z), part_cols(z, mine_at)]
         spread = [send(here, here, at(z_=(z + k) % nz)) for k in range(1, nz)]
+        other.wait_recv()
+
+        def combine(t, carry):
+            c = columns(t * tile, tile)
+            field_high, field_low = halves(
+                fields[m, :, columns(mine_at + t * tile, tile)]
+                + from_core[m, :, c]
+            )
+            high[m, 0:rows, c] = field_high
+            low[m, 0:rows, c] = field_low
+            return carry
+
+        lax.fori_loop(0, half // tile, combine, 0)
         yield
         for copy in spread:
             copy.wait_recv()
@@ -246,35 +285,27 @@
         for first in (0, 1):
             for n in range(2):
                 h = 1 - n if first == 0 else n
-                here = full.at[m, mine, side[h]]
+                here = full.at[m, mine, full_side(h)]
                 gathered[n, h] = send(here, here, at(x_=(x1, x3)[n]))
-        here = full.at[m, mine, :]
-        shared = [send(here, here, at(core_=1 - core))]
         yield
         for n in range(2):
             h = 1 - n
             gathered[n, h].wait_recv()
-            here = full.at[m, group_rows((x1, x3)[n]), side[h]]
+            here = full.at[m, group_rows((x1, x3)[n]), full_side(h)]
             gathered[2, h] = send(here, here, at(x_=(x3, x1)[n]))
         yield
-        for n in range(2):
-            gathered[n, n].wait_recv()
-            here = full.at[m, group_rows((x1, x3)[n]), :]
-            shared.append(send(here, here, at(core_=1 - core)))
-        for h in range(2):
-            gathered[2, h].wait_recv()
-            here = full.at[m, group_rows(x2), side[h]]
-            shared.append(send(here, here, at(core_=1 - core)))
-        yield
-        for copy in shared:
-            copy.wait_recv()
-        value_high, value_low = halves(full[m])
-        left_out[m, :rank] = value_high
-        left_out[m, rank:] = value_low
+        for n, h in ((0, 0), (1, 1), (2, 0), (2, 1)):
+            gathered[n, h].wait_recv()
+        c = columns(mine_at, half)
+        here = full.at[m, :, c]
+        shared.append(send(here, here, at(core_=1 - core)))
+        value_high, value_low = halves(full[m, :, c])
+        left_out[m, :rank, c] = value_high
+        left_out[m, rank:, c] = value_low
         high[m, rows : rows + rank, :] = value_high
         low[m, rows : rows + rank, :] = value_low
         total = jnp.zeros((rows + rank, 2 * rank), F32)
-        for t in range(cols // depth):
+        for t in range(half // depth):
             c = pl.ds(t * depth, depth)
             left_high = high[m, rows : rows + rank, c]
             left_low = low[m, rows : rows + rank, c]
@@ -294,17 +325,14 @@
         totals[m] = total
 
     streams = (stream(0), stream(1))
-    for m in (0, 0, 1, 0, 0, 1, 1, 0, 1, 0, 1, 1, 0, 1, 0, 1, 0, 1, 0, 0, 1, 1):
+    for m in (0, 0, 1, 1, 0, 0, 1, 1) + (0, 1) * 6:
         next(streams[m], None)
 
     lane = lax.broadcasted_iota(jnp.int32, (1, 2 * rank), 1)
     packed = jnp.where(lane < rank, totals[0], totals[1])
     gram[...] = packed[rows:]
-    gram_all[y] = packed[rows:]
     prod[...] = packed[:rows]
-    gram_copies = [
-        send(gram, gram_all.at[y], at(y_=(y + k) % ny)) for k in range(1, ny)
-    ]
+    gram_pair = send(gram, gram_core, at(core_=1 - core))
 
     def share_rows(o):
         return pl.ds(pl.multiple_of(o * share, share), share)
@@ -314,6 +342,12 @@
         o, device = owner_at(k)
         rs_copies.append(send(prod.at[share_rows(o), :], prod_rs.at[k], device))
 
+    gram_pair.wait_recv()
+    gram_all[y] = gram[...] + gram_core[...]
+    gram_copies = [
+        send(gram_all.at[y], gram_all.at[y], at(y_=(y + k) % ny))
+        for k in range(1, ny)
+    ]
     total = prod[share_rows(owner), :]
     for k in range(1, owners):
         rs_copies[k - 1].wait_recv()
@@ -336,22 +370,32 @@
     elim[0] = jnp.where(col < rank, gram_sum, unit)
     elim[1] = jnp.where(col < rank, pltpu.roll(gram_sum, rank, 1), unit)
 
-    def step(k, carry):
+    def entry(value, n):
+        return jnp.sum(jnp.where(lane == n, value, 0.0), axis=1, keepdims=True)
+
+    def step(j, carry):
+        k = 2 * j
         for m in range(2):
             value = elim[m]
-            pivot_row = elim[m, pl.ds(k, 1), :]
-            pick = col == k
-            pivot_col = jnp.sum(
-                jnp.where(pick, value, 0.0), axis=1, keepdims=True
-            )
-            pivot = jnp.sum(
-                jnp.where(lane == k, pivot_row, 0.0), axis=1, keepdims=True
-            )
-            factor = jnp.where(row[:, :1] > k, pivot_col / pivot, 0.0)
-            elim[m] = value - factor * pivot_row
+            row_one = elim[m, pl.ds(k, 1), :]
+            row_two = elim[m, pl.ds(k + 1, 1), :]
+            col_one, col_two = entry(value, k), entry(value, k + 1)
+            pivot_one, above = entry(row_one, k), entry(row_one, k + 1)
+            below, pivot_two = entry(row_two, k), entry(row_two, k + 1)
+            inverse = 1.0 / pivot_one
+            ratio = below * inverse
+            row_two = row_two - ratio * row_one
+            pivot_two = pivot_two - ratio * above
+            one = jnp.where(row[:, :1] > k, col_one * inverse, 0.0)
+            two = jnp.where(
+                row[:, :1] > k + 1,
+                (col_two - one * above) * (1.0 / pivot_two),
+                0.0,
+            )
+            elim[m] = value - one * row_one - two * row_two
         return carry
 
-    cuts = [0, 5 * rank // 16, 3 * rank // 4, rank]
+    cuts = [0, 5 * rank // 32, 3 * rank // 8, rank // 2]
 
     def eliminate(n):
         lax.fori_loop(cuts[n], cuts[n + 1], step, 0)
@@ -385,9 +429,14 @@
             jnp.where(row == col, value, 0.0), axis=1, keepdims=True
         )
         scaled.append(value / jnp.sqrt(pivots))
-    inv_out[...] = jnp.where(
-        lane < rank, pltpu.roll(scaled[0], rank, 1), scaled[1]
-    )
+    inv_out[:rank] = jnp.where(lane < rank, pltpu.roll(scaled[0], rank, 1), 0.0)
+    inv_out[rank:] = jnp.where(lane < rank, 0.0, scaled[1])
+    for m in range(2):
+        shared[m].wait_recv()
+        c = columns(other_at, half)
+        value_high, value_low = halves(full[m, :, c])
+        left_out[m, :rank, c] = value_high
+        left_out[m, rank:, c] = value_low
     for copy in copies:
         copy.wait_recv()
     prod_out[...] = prod_full[...]
@@ -401,14 +450,16 @@
     ny, nz = sizes
     rows, cols = grad_in.shape
     rank = warm_in.shape[0]
-    half_rank = rank // CORES
-    group = half_rank // NX
+    group = rank // NX
+    half = cols // CORES
+    part_rows = 8
+    part = half * group // (part_rows * nz)
     owners = ny * CORES
     share = rows // owners
     hbm = pl.BlockSpec(memory_space=pltpu.HBM)
     vmem = pl.BlockSpec(memory_space=pltpu.VMEM)
     smem = pl.BlockSpec(memory_space=pltpu.SMEM)
-    count = 2 * (2 + 6 + 2 * (nz - 1) + 6 + 5)
+    count = 2 * (2 + 6 + 2 * (nz - 1) + 6 + 2) + 1
     count += (ny - 1) + 2 * (owners - 1) + (NX - 1) + (nz - 1)
     return pl.pallas_call(
         functools.partial(reduce_kernel, sizes),
@@ -416,7 +467,7 @@
             pltpu.VMEM((2, rows, cols), F32),
             pltpu.VMEM((2, 2 * rank, cols), BF16),
             pltpu.VMEM((rows, 2 * rank), F32),
-            pltpu.VMEM((rank, 2 * rank), F32),
+            pltpu.VMEM((2 * rank, 2 * rank), F32),
         ),
         in_specs=[hbm] * 6 + [smem],
         out_specs=(vmem,) * 4,
@@ -424,14 +475,17 @@
             pltpu.VMEM((2, rows, cols), BF16),
             pltpu.VMEM((2, rows, cols), F32),
             pltpu.VMEM((2, rank, rows), F32),
-            pltpu.VMEM((2, rows + rank, cols), BF16),
-            pltpu.VMEM((2, rows + rank, cols), BF16),
+            pltpu.VMEM((2, rows + rank, half), BF16),
+            pltpu.VMEM((2, rows + rank, half), BF16),
+            pltpu.VMEM((2, rank, half), F32),
+            pltpu.VMEM((2, rank, half), F32),
+            pltpu.VMEM((2, rank, half), F32),
+            pltpu.VMEM((2, rows, half), F32),
+            pltpu.VMEM((2, 2, group, half), F32),
+            pltpu.VMEM((2, group, half), F32),
+            pltpu.VMEM((2, nz, part_rows, part), F32),
             pltpu.VMEM((2, rank, cols), F32),
-            pltpu.VMEM((2, half_rank, cols), F32),
-            pltpu.VMEM((2, 2, group, cols), F32),
-            pltpu.VMEM((2, group, cols), F32),
-            pltpu.VMEM((2, nz, group, cols // nz), F32),
-            pltpu.VMEM((2, rank, cols), F32),
+            pltpu.VMEM((rank, 2 * rank), F32),
             pltpu.VMEM((rank, 2 * rank), F32),
             pltpu.VMEM((ny, rank, 2 * rank), F32),
             pltpu.VMEM((rows, 2 * rank), F32),
@@ -442,7 +496,7 @@
             pltpu.VMEM((2, rank, 2 * rank), F32),
             pltpu.SemaphoreType.DMA((count,)),
             pltpu.SemaphoreType.DMA((count,)),
-            pltpu.SemaphoreType.DMA((2, 2, 2)),
+            pltpu.SemaphoreType.DMA((2, 2, 2, 2)),
             pltpu.SemaphoreType.DMA((2,)),
         ],
         compiler_params=pltpu.CompilerParams(
@@ -469,41 +523,45 @@
     store_sems,
 ):
     rows, cols = fields.shape[1:]
-    rank = inv.shape[0]
+    rank = inv.shape[0] // 2
     tile = made.shape[-1]
     exact = functools.partial(
         lax.dot_general,
         precision=lax.Precision.HIGHEST,
         preferred_element_type=F32,
     )
+    inverse = inv[...]
+    product = prod[...] * (1.0 / replicas)
+    warm = exact(product, inverse, (((1,), (1,)), ((), ())))
+    applied = exact(warm, inverse, (((1,), (0,)), ((), ())))
+    lane = lax.broadcasted_iota(jnp.int32, (1, 2 * rank), 1)
+    for m in range(2):
+        own = jnp.where(lane // rank == m, applied, 0.0)
+        moved = pltpu.roll(own, rank, 1)
+        twice = (own + moved).astype(BF16)
+        rest = halves((own, moved)[m])[1]
+        factor[m] = jnp.concatenate([twice, rest], axis=1)
     stores = []
-    for m, warm_out in enumerate((new_warm_in, new_warm_out)):
-        lanes = slice(m * rank, (m + 1) * rank)
-        inverse = inv[:, lanes]
-        warm = exact(inverse, prod[:, lanes], (((1,), (1,)), ((), ()))) / replicas
-        warm_out[...] = warm
-        applied = exact(warm, inverse, (((0,), (0,)), ((), ())))
-        applied_high, applied_low = halves(applied)
-        factor[m] = jnp.concatenate(
-            [applied_high, applied_high, applied_low], axis=1
-        )
     for m, out in enumerate((new_error_in, new_error_out)):
         for t in range(cols // tile):
             c = pl.ds(t * tile, tile)
-            stacked = jnp.concatenate([left[m, :, c], left[m, :rank, c]], axis=0)
+            stacked = jnp.concatenate([left[m, :, c], left[m, :, c]], axis=0)
             made[m, t] = fields[m, :, c] - dot(factor[m], stacked, 1, 0)
             store = pltpu.make_async_copy(
                 made.at[m, t], out.at[:, c], store_sems.at[m, t]
             )
             store.start()
             stores.append(store)
+    both = exact(inverse, product, (((1,), (1,)), ((), ())))
+    new_warm_in[...] = both[:rank]
+    new_warm_out[...] = both[rank:]
     for store in stores:
         store.wait()
 
 
 def finish_call(replicas, fields, left, prod, inv):
     rows, cols = fields.shape[1:]
-    rank = inv.shape[0]
+    rank = inv.shape[0] // 2
     tile = min(512, cols)
     vmem = pl.BlockSpec(memory_space=pltpu.VMEM)
     hbm = pl.BlockSpec(memory_space=pltpu.HBM)
@@ -518,7 +576,7 @@
         in_specs=[vmem] * 4,
         out_specs=(hbm, hbm, vmem, vmem),
         scratch_shapes=[
-            pltpu.VMEM((2, rows, 3 * rank), BF16),
+            pltpu.VMEM((2, rows, 4 * rank), BF16),
             pltpu.VMEM((2, cols // tile, rows, tile), F32),
             pltpu.SemaphoreType.DMA((2, cols // tile)),
         ],

time: 68.9 us -> 66.5 us (0.965)
  Pallas kernels: 67.5 us -> 65.1 us
    pallas_call x1, Pallas kernels: 63.1 us -> 61.3 us  [reduce_call(): pl.pallas_call(functools.partial(reduce_kernel, sizes), out_shape=(pltpu....]
where the time goes in v3:
time: 66.5 us; the launch traced here: 66.4 us
  Pallas kernels  65.1 us (98%)
  between operations  1.29 us (2%)
    pallas_call x1, Pallas kernels, reduce_call(): pl.pallas_call(functools.partial(reduce_kernel, sizes), out_shape=(pltpu....  61.3 us
    pallas_call x1, Pallas kernels, finish_call(): pl.pallas_call(functools.partial(finish_kernel, replicas), out_shape=(jax...  3.81 us

profile of v3, /device:TPU:1, one launch (start us, length us, event | category | flops | bytes accessed | tf_op | source)
XLA Modules:
  0.0 66.4 jit_solution(2119744496605445975)
XLA Ops:
  1.3 61.3 %reduce_left.1 = (f32[2,192,3072]{2,1,0:T(8,128)S(1)}, bf16[2,128,3072]{2,1,0:T(8,128)(2,1)S(1)}, f32[192,128]{1,0:T(8,128)S(1)}, f32[128,128]{1,0:T(8,128)S(1)}) custom-call(bf16[192,3072]{1,0:T(8,128)(2,1)} %bitcast.14, bf16[192,3072]{1,0:T(8,128)(2,1)} %bitcast.15, f32[192,3072]{1,0:T(8,128)} %bitcast.12, f32[192,3072]{1,0:T(8,128)} %bitcast.13, ...), custom_call_target="tpu_custom_call" | custom-call | tf_op jit(solution)/shard_map/reduce_left/pallas_call | solution.py:464
  62.5 3.8 %new_errors.1 = (f32[192,3072]{1,0:T(8,128)}, f32[192,3072]{1,0:T(8,128)}, f32[64,192]{1,0:T(8,128)}, f32[64,192]{1,0:T(8,128)}) custom-call(f32[2,192,3072]{2,1,0:T(8,128)S(1)} %get-tuple-element.12.fields, bf16[2,128,3072]{2,1,0:T(8,128)(2,1)S(1)} %get-tuple-element.13.left, f32[192,128]{1,0:T(8,128)S(1)} %get-tuple-element.14.prod, ...), custom_call_target="tpu_custom_call" | custom-call | tf_op jit(solution)/shard_map/new_errors/pallas_call | solution.py:568

commit v4 on v3

--- a/solution.py
+++ b/solution.py
@@ -24,6 +24,20 @@
     return lax.dot_general(
         a, b, (((dim_a,), (dim_b,)), ((), ())), preferred_element_type=F32
     )
+
+
+def exact(a, b, dim_a, dim_b):
+    return lax.dot_general(
+        a,
+        b,
+        (((dim_a,), (dim_b,)), ((), ())),
+        precision=lax.Precision.HIGHEST,
+        preferred_element_type=F32,
+    )
+
+
+def farthest_first(n):
+    return sorted(range(1, n), key=lambda k: -min(k, n - k))
 
 
 def reciprocal_of(scale_ref):
@@ -100,6 +114,13 @@
         o = (owner + k) % owners
         return o, at(core_=o % CORES, y_=o // CORES)
 
+    peers = [at(z_=(z + k) % nz) for k in farthest_first(nz)]
+    peers += [at(x_=(x + k) % NX) for k in farthest_first(NX)]
+    peers += [owner_at(k)[1] for k in farthest_first(owners)]
+    barrier = pltpu.get_barrier_semaphore()
+    for peer in peers:
+        pl.semaphore_signal(barrier, inc=1, device_id=peer, device_id_type=MESH)
+
     mine_at = core * half
     other_at = (1 - core) * half
 
@@ -121,13 +142,6 @@
                     copy.start()
                     loads[m, b, h, a] = copy
 
-    peers = [at(x_=(x + k) % NX) for k in range(1, NX)]
-    peers += [at(z_=(z + k) % nz) for k in range(1, nz)]
-    peers += [owner_at(k)[1] for k in range(1, owners)]
-    barrier = pltpu.get_barrier_semaphore()
-    for peer in peers:
-        pl.semaphore_signal(barrier, inc=1, device_id=peer, device_id_type=MESH)
-
     number = itertools.count()
     sent = []
 
@@ -162,7 +176,7 @@
     def part_cols(z_, start=0):
         return columns(start + z_ % across * part, part)
 
-    tile = min(384, piece)
+    tile = min(768, piece)
     depth = min(768, half)
     totals = [None, None]
     shared = []
@@ -255,16 +269,19 @@
                 from_z.at[m, k],
                 at(z_=(z + k) % nz),
             )
-            for k in range(1, nz)
+            for k in farthest_first(nz)
         ]
         yield
+        for copy in summed:
+            copy.wait_recv()
         total = left[m, part_rows_of(x, z), part_cols(z)]
         for k in range(1, nz):
-            summed[k - 1].wait_recv()
             total += from_z[m, k]
         full[m, part_rows_of(x, z), part_cols(z, mine_at)] = total
         here = full.at[m, part_rows_of(x, z), part_cols(z, mine_at)]
-        spread = [send(here, here, at(z_=(z + k) % nz)) for k in range(1, nz)]
+        spread = [
+            send(here, here, at(z_=(z + k) % nz)) for k in farthest_first(nz)
+        ]
         other.wait_recv()
 
         def combine(t, carry):
@@ -297,8 +314,6 @@
         for n, h in ((0, 0), (1, 1), (2, 0), (2, 1)):
             gathered[n, h].wait_recv()
         c = columns(mine_at, half)
-        here = full.at[m, :, c]
-        shared.append(send(here, here, at(core_=1 - core)))
         value_high, value_low = halves(full[m, :, c])
         left_out[m, :rank, c] = value_high
         left_out[m, rank:, c] = value_low
@@ -325,7 +340,7 @@
         totals[m] = total
 
     streams = (stream(0), stream(1))
-    for m in (0, 0, 1, 1, 0, 0, 1, 1) + (0, 1) * 6:
+    for m in (0, 0, 1, 0, 0, 1, 1, 1) + (0, 1) * 6:
         next(streams[m], None)
 
     lane = lax.broadcasted_iota(jnp.int32, (1, 2 * rank), 1)
@@ -338,7 +353,7 @@
         return pl.ds(pl.multiple_of(o * share, share), share)
 
     rs_copies = []
-    for k in range(1, owners):
+    for k in farthest_first(owners):
         o, device = owner_at(k)
         rs_copies.append(send(prod.at[share_rows(o), :], prod_rs.at[k], device))
 
@@ -346,17 +361,22 @@
     gram_all[y] = gram[...] + gram_core[...]
     gram_copies = [
         send(gram_all.at[y], gram_all.at[y], at(y_=(y + k) % ny))
-        for k in range(1, ny)
+        for k in farthest_first(ny)
     ]
+    for copy in rs_copies:
+        copy.wait_recv()
     total = prod[share_rows(owner), :]
     for k in range(1, owners):
-        rs_copies[k - 1].wait_recv()
         total += prod_rs[k]
     prod_x[x] = total
     copies = [
         send(prod_x.at[x], prod_x.at[x], at(x_=(x + k) % NX))
-        for k in range(1, NX)
+        for k in farthest_first(NX)
     ]
+
+    for m in range(2):
+        here = full.at[m, :, columns(mine_at, half)]
+        shared.append(send(here, here, at(core_=1 - core)))
 
     for copy in gram_copies:
         copy.wait_recv()
@@ -409,7 +429,7 @@
     prod_z[z] = total
     copies = [
         send(prod_z.at[z], prod_z.at[z], at(z_=(z + k) % nz))
-        for k in range(1, nz)
+        for k in farthest_first(nz)
     ]
     eliminate(1)
     for copy in copies:
@@ -419,7 +439,7 @@
         total += prod_z[k]
     prod_full[share_rows(owner), :] = total
     here = prod_full.at[share_rows(owner), :]
-    copies = [send(here, here, owner_at(k)[1]) for k in range(1, owners)]
+    copies = [send(here, here, owner_at(k)[1]) for k in farthest_first(owners)]
     eliminate(2)
 
     scaled = []
@@ -429,8 +449,15 @@
             jnp.where(row == col, value, 0.0), axis=1, keepdims=True
         )
         scaled.append(value / jnp.sqrt(pivots))
-    inv_out[:rank] = jnp.where(lane < rank, pltpu.roll(scaled[0], rank, 1), 0.0)
-    inv_out[rank:] = jnp.where(lane < rank, 0.0, scaled[1])
+    inverse = jnp.concatenate(
+        [
+            jnp.where(lane < rank, pltpu.roll(scaled[0], rank, 1), 0.0),
+            jnp.where(lane < rank, 0.0, scaled[1]),
+        ],
+        axis=0,
+    )
+    inv_out[0] = inverse
+    inv_out[1] = exact(inverse, inverse, 0, 0)
     for m in range(2):
         shared[m].wait_recv()
         c = columns(other_at, half)
@@ -467,7 +494,7 @@
             pltpu.VMEM((2, rows, cols), F32),
             pltpu.VMEM((2, 2 * rank, cols), BF16),
             pltpu.VMEM((rows, 2 * rank), F32),
-            pltpu.VMEM((2 * rank, 2 * rank), F32),
+            pltpu.VMEM((2, 2 * rank, 2 * rank), F32),
         ),
         in_specs=[hbm] * 6 + [smem],
         out_specs=(vmem,) * 4,
@@ -523,17 +550,10 @@
     store_sems,
 ):
     rows, cols = fields.shape[1:]
-    rank = inv.shape[0] // 2
+    rank = inv.shape[1] // 2
     tile = made.shape[-1]
-    exact = functools.partial(
-        lax.dot_general,
-        precision=lax.Precision.HIGHEST,
-        preferred_element_type=F32,
-    )
-    inverse = inv[...]
     product = prod[...] * (1.0 / replicas)
-    warm = exact(product, inverse, (((1,), (1,)), ((), ())))
-    applied = exact(warm, inverse, (((1,), (0,)), ((), ())))
+    applied = exact(product, inv[1], 1, 0)
     lane = lax.broadcasted_iota(jnp.int32, (1, 2 * rank), 1)
     for m in range(2):
         own = jnp.where(lane // rank == m, applied, 0.0)
@@ -552,7 +572,7 @@
             )
             store.start()
             stores.append(store)
-    both = exact(inverse, product, (((1,), (1,)), ((), ())))
+    both = exact(inv[0], product, 1, 1)
     new_warm_in[...] = both[:rank]
     new_warm_out[...] = both[rank:]
     for store in stores:
@@ -561,7 +581,7 @@
 
 def finish_call(replicas, fields, left, prod, inv):
     rows, cols = fields.shape[1:]
-    rank = inv.shape[0] // 2
+    rank = inv.shape[1] // 2
     tile = min(512, cols)
     vmem = pl.BlockSpec(memory_space=pltpu.VMEM)
     hbm = pl.BlockSpec(memory_space=pltpu.HBM)

time: 66.5 us -> 62 us (0.932)
  Pallas kernels: 65.1 us -> 60.6 us
    pallas_call x1, Pallas kernels: 61.3 us -> 57.1 us  [reduce_call(): pl.pallas_call(functools.partial(reduce_kernel, sizes), out_shape=(pltpu....]
where the time goes in v4:
time: 62 us; the launch traced here: 61.9 us
  Pallas kernels  60.6 us (98%)
  between operations  1.29 us (2%)
    pallas_call x1, Pallas kernels, reduce_call(): pl.pallas_call(functools.partial(reduce_kernel, sizes), out_shape=(pltpu....  57.1 us
    pallas_call x1, Pallas kernels, finish_call(): pl.pallas_call(functools.partial(finish_kernel, replicas), out_shape=(jax...  3.5 us

profile of v4, /device:TPU:1, one launch (start us, length us, event | category | flops | bytes accessed | tf_op | source)
XLA Modules:
  0.0 61.9 jit_solution(3481995085564878663)
XLA Ops:
  1.3 57.1 %reduce_left.1 = (f32[2,192,3072]{2,1,0:T(8,128)S(1)}, bf16[2,128,3072]{2,1,0:T(8,128)(2,1)S(1)}, f32[192,128]{1,0:T(8,128)S(1)}, f32[2,128,128]{2,1,0:T(8,128)S(1)}) custom-call(bf16[192,3072]{1,0:T(8,128)(2,1)} %bitcast.14, bf16[192,3072]{1,0:T(8,128)(2,1)} %bitcast.15, f32[192,3072]{1,0:T(8,128)} %bitcast.12, f32[192,3072]{1,0:T(8,128)} %bitcast.13, ...), custom_call_target="tpu_custom_call" | custom-call | tf_op jit(solution)/shard_map/reduce_left/pallas_call | solution.py:491
  58.4 3.5 %new_errors.1 = (f32[192,3072]{1,0:T(8,128)}, f32[192,3072]{1,0:T(8,128)}, f32[64,192]{1,0:T(8,128)}, f32[64,192]{1,0:T(8,128)}) custom-call(f32[2,192,3072]{2,1,0:T(8,128)S(1)} %get-tuple-element.12.fields, bf16[2,128,3072]{2,1,0:T(8,128)(2,1)S(1)} %get-tuple-element.13.left, f32[192,128]{1,0:T(8,128)S(1)} %get-tuple-element.14.prod, ...), custom_call_target="tpu_custom_call" | custom-call | tf_op jit(solution)/shard_map/new_errors/pallas_call | solution.py:588

commit v5 on v4

--- a/solution.py
+++ b/solution.py
@@ -180,6 +180,7 @@
     depth = min(768, half)
     totals = [None, None]
     shared = []
+    others = [None, None]
 
     def stream(m):
         exchanged = []
@@ -253,7 +254,7 @@
                     at(x_=(x3, x1)[h]),
                 )
             )
-        other = send(
+        others[m] = send(
             fields.at[m, :, columns(other_at, half)],
             from_core.at[m],
             at(core_=1 - core),
@@ -282,19 +283,6 @@
         spread = [
             send(here, here, at(z_=(z + k) % nz)) for k in farthest_first(nz)
         ]
-        other.wait_recv()
-
-        def combine(t, carry):
-            c = columns(t * tile, tile)
-            field_high, field_low = halves(
-                fields[m, :, columns(mine_at + t * tile, tile)]
-                + from_core[m, :, c]
-            )
-            high[m, 0:rows, c] = field_high
-            low[m, 0:rows, c] = field_low
-            return carry
-
-        lax.fori_loop(0, half // tile, combine, 0)
         yield
         for copy in spread:
             copy.wait_recv()
@@ -339,9 +327,32 @@
             total += one + pltpu.roll(one, rank, 1) + two
         totals[m] = total
 
+    def combine(m):
+        others[m].wait_recv()
+
+        def one(t, carry):
+            c = columns(t * tile, tile)
+            field_high, field_low = halves(
+                fields[m, :, columns(mine_at + t * tile, tile)]
+                + from_core[m, :, c]
+            )
+            high[m, 0:rows, c] = field_high
+            low[m, 0:rows, c] = field_low
+            return carry
+
+        lax.fori_loop(0, half // tile, one, 0)
+
     streams = (stream(0), stream(1))
-    for m in (0, 0, 1, 0, 0, 1, 1, 1) + (0, 1) * 6:
-        next(streams[m], None)
+
+    def advance(order):
+        for m in order:
+            next(streams[m], None)
+
+    advance((0, 0, 1, 0, 0, 1, 1, 1) + (0, 1) * 2)
+    combine(0)
+    advance((0, 1))
+    combine(1)
+    advance((0, 1) * 3)
 
     lane = lax.broadcasted_iota(jnp.int32, (1, 2 * rank), 1)
     packed = jnp.where(lane < rank, totals[0], totals[1])
@@ -415,7 +426,7 @@
             elim[m] = value - one * row_one - two * row_two
         return carry
 
-    cuts = [0, 5 * rank // 32, 3 * rank // 8, rank // 2]
+    cuts = [0, 3 * rank // 64, 19 * rank // 64, rank // 2]
 
     def eliminate(n):
         lax.fori_loop(cuts[n], cuts[n + 1], step, 0)
@@ -432,6 +443,9 @@
         for k in farthest_first(nz)
     ]
     eliminate(1)
+    early, sent[:] = sent[:], []
+    for copy in early:
+        copy.wait_send()
     for copy in copies:
         copy.wait_recv()
     total = prod_z[0]
@@ -547,7 +561,9 @@
     new_warm_out,
     factor,
     made,
+    warms,
     store_sems,
+    warm_sems,
 ):
     rows, cols = fields.shape[1:]
     rank = inv.shape[1] // 2
@@ -563,6 +579,15 @@
         factor[m] = jnp.concatenate([twice, rest], axis=1)
     stores = []
     for m, out in enumerate((new_error_in, new_error_out)):
+        if m == 1:
+            both = exact(inv[0], product, 1, 1)
+            for n, warm_out in enumerate((new_warm_in, new_warm_out)):
+                warms[n] = both[n * rank : (n + 1) * rank]
+                store = pltpu.make_async_copy(
+                    warms.at[n], warm_out, warm_sems.at[n]
+                )
+                store.start()
+                stores.append(store)
         for t in range(cols // tile):
             c = pl.ds(t * tile, tile)
             stacked = jnp.concatenate([left[m, :, c], left[m, :, c]], axis=0)
@@ -572,9 +597,6 @@
             )
             store.start()
             stores.append(store)
-    both = exact(inv[0], product, 1, 1)
-    new_warm_in[...] = both[:rank]
-    new_warm_out[...] = both[rank:]
     for store in stores:
         store.wait()
 
@@ -594,11 +616,13 @@
             jax.ShapeDtypeStruct((rank, rows), F32),
         ),
         in_specs=[vmem] * 4,
-        out_specs=(hbm, hbm, vmem, vmem),
+        out_specs=(hbm,) * 4,
         scratch_shapes=[
             pltpu.VMEM((2, rows, 4 * rank), BF16),
             pltpu.VMEM((2, cols // tile, rows, tile), F32),
+            pltpu.VMEM((2, rank, rows), F32),
             pltpu.SemaphoreType.DMA((2, cols // tile)),
+            pltpu.SemaphoreType.DMA((2,)),
         ],
         compiler_params=pltpu.CompilerParams(
             vmem_limit_bytes=32 * 1024 * 1024,

time: 62 us -> 61.2 us (0.987)
  Pallas kernels: 60.6 us -> 59.8 us
where the time goes in v5:
time: 61.2 us; the launch traced here: 61.1 us
  Pallas kernels  59.8 us (98%)
  between operations  1.29 us (2%)
    pallas_call x1, Pallas kernels, reduce_call(): pl.pallas_call(functools.partial(reduce_kernel, sizes), out_shape=(pltpu....  56.9 us
    pallas_call x1, Pallas kernels, finish_call(): pl.pallas_call(functools.partial(finish_kernel, replicas), out_shape=(jax...  2.92 us

profile of v5, /device:TPU:1, one launch (start us, length us, event | category | flops | bytes accessed | tf_op | source)
XLA Modules:
  0.0 61.1 jit_solution(17508784478031751085)
XLA Ops:
  1.3 56.9 %reduce_left.1 = (f32[2,192,3072]{2,1,0:T(8,128)S(1)}, bf16[2,128,3072]{2,1,0:T(8,128)(2,1)S(1)}, f32[192,128]{1,0:T(8,128)S(1)}, f32[2,128,128]{2,1,0:T(8,128)S(1)}) custom-call(bf16[192,3072]{1,0:T(8,128)(2,1)} %bitcast.14, bf16[192,3072]{1,0:T(8,128)(2,1)} %bitcast.15, f32[192,3072]{1,0:T(8,128)} %bitcast.12, f32[192,3072]{1,0:T(8,128)} %bitcast.13, ...), custom_call_target="tpu_custom_call" | custom-call | tf_op jit(solution)/shard_map/reduce_left/pallas_call | solution.py:505
  58.2 2.9 %new_errors.1 = (f32[192,3072]{1,0:T(8,128)}, f32[192,3072]{1,0:T(8,128)}, f32[64,192]{1,0:T(8,128)}, f32[64,192]{1,0:T(8,128)}) custom-call(f32[2,192,3072]{2,1,0:T(8,128)S(1)} %get-tuple-element.12.fields, bf16[2,128,3072]{2,1,0:T(8,128)(2,1)S(1)} %get-tuple-element.13.left, f32[192,128]{1,0:T(8,128)S(1)} %get-tuple-element.14.prod, ...), custom_call_target="tpu_custom_call" | custom-call | tf_op jit(solution)/shard_map/new_errors/pallas_call | solution.py:610

commit v6 on v5

--- a/solution.py
+++ b/solution.py
@@ -177,7 +177,7 @@
         return columns(start + z_ % across * part, part)
 
     tile = min(768, piece)
-    depth = min(768, half)
+    depth = min(384, half)
     totals = [None, None]
     shared = []
     others = [None, None]
@@ -358,7 +358,6 @@
     packed = jnp.where(lane < rank, totals[0], totals[1])
     gram[...] = packed[rows:]
     prod[...] = packed[:rows]
-    gram_pair = send(gram, gram_core, at(core_=1 - core))
 
     def share_rows(o):
         return pl.ds(pl.multiple_of(o * share, share), share)
@@ -368,6 +367,7 @@
         o, device = owner_at(k)
         rs_copies.append(send(prod.at[share_rows(o), :], prod_rs.at[k], device))
 
+    gram_pair = send(gram, gram_core, at(core_=1 - core))
     gram_pair.wait_recv()
     gram_all[y] = gram[...] + gram_core[...]
     gram_copies = [

time: 61.2 us -> 61.2 us (level)
  no operation moved by 1% of the time
where the time goes in v6:
time: 61.2 us; the launch traced here: 61.1 us
  Pallas kernels  59.8 us (98%)
  between operations  1.29 us (2%)
    pallas_call x1, Pallas kernels, reduce_call(): pl.pallas_call(functools.partial(reduce_kernel, sizes), out_shape=(pltpu....  56.9 us
    pallas_call x1, Pallas kernels, finish_call(): pl.pallas_call(functools.partial(finish_kernel, replicas), out_shape=(jax...  2.92 us

profile of v6, /device:TPU:1, one launch (start us, length us, event | category | flops | bytes accessed | tf_op | source)
XLA Modules:
  0.0 61.1 jit_solution(5400109425183356730)
XLA Ops:
  1.3 56.9 %reduce_left.1 = (f32[2,192,3072]{2,1,0:T(8,128)S(1)}, bf16[2,128,3072]{2,1,0:T(8,128)(2,1)S(1)}, f32[192,128]{1,0:T(8,128)S(1)}, f32[2,128,128]{2,1,0:T(8,128)S(1)}) custom-call(bf16[192,3072]{1,0:T(8,128)(2,1)} %bitcast.14, bf16[192,3072]{1,0:T(8,128)(2,1)} %bitcast.15, f32[192,3072]{1,0:T(8,128)} %bitcast.12, f32[192,3072]{1,0:T(8,128)} %bitcast.13, ...), custom_call_target="tpu_custom_call" | custom-call | tf_op jit(solution)/shard_map/reduce_left/pallas_call | solution.py:505
  58.2 2.9 %new_errors.1 = (f32[192,3072]{1,0:T(8,128)}, f32[192,3072]{1,0:T(8,128)}, f32[64,192]{1,0:T(8,128)}, f32[64,192]{1,0:T(8,128)}) custom-call(f32[2,192,3072]{2,1,0:T(8,128)S(1)} %get-tuple-element.12.fields, bf16[2,128,3072]{2,1,0:T(8,128)(2,1)S(1)} %get-tuple-element.13.left, f32[192,128]{1,0:T(8,128)S(1)} %get-tuple-element.14.prod, ...), custom_call_target="tpu_custom_call" | custom-call | tf_op jit(solution)/shard_map/new_errors/pallas_call | solution.py:610
